TPU v7x, 32 devices: a whole 2x2x4 slice. The times are simulated.
32 devices in a mesh: pipe: 2 (over x), dp: 16 (over z, y, core).
Axes of the slice: x: 2, y: 2, z: 4, core: 2. Of those that a mesh axis runs over, the one named last changes fastest.
Arguments:
- content_ends: bfloat16 [2, 4096, 768], P('pipe', 'dp'), may hold values from -6 to 6
- query_ends: bfloat16 [2, 512, 768], P('pipe', 'dp'), may hold values from -6 to 6
- w_query: bfloat16 [2, 768, 768], P('pipe'), may hold values from -0.21875 to 0.21875
- b_query: float32 [2, 768], P('pipe'), may hold values from -4 to 4
- w_key: bfloat16 [2, 768, 768], P('pipe'), may hold values from -0.21875 to 0.21875
- w_value: bfloat16 [2, 768, 768], P('pipe'), may hold values from -0.21875 to 0.21875
- b_value: float32 [2, 768], P('pipe'), may hold values from -4 to 4
- w_out: bfloat16 [2, 768, 768], P('pipe'), may hold values from -0.875 to 0.875
- b_out: float32 [2, 768], P('pipe'), may hold values from -4 to 4
- gain_attn: float32 [2, 768], P('pipe'), may hold values from 0.25 to 1.75
- shift_attn: float32 [2, 768], P('pipe'), may hold values from -4 to 4
- w_up: bfloat16 [2, 768, 3072], P('pipe'), may hold values from -0.21875 to 0.21875
- b_up: float32 [2, 3072], P('pipe'), may hold values from -4 to 4
- w_down: bfloat16 [2, 3072, 768], P('pipe'), may hold values from -0.109375 to 0.109375
- b_down: float32 [2, 768], P('pipe'), may hold values from -4 to 4
- gain_ffn: float32 [2, 768], P('pipe'), may hold values from 0.25 to 1.75
- shift_ffn: float32 [2, 768], P('pipe'), may hold values from -4 to 4
- rel_table: float32 [2, 32, 12], P('pipe'), may hold values from -6 to 6
- doc_lengths: int32 [32, 4], P('dp'), may hold values from 1 to 96, 128 in all within a row
- position_order: int32 [32, 128], P('dp'), may hold values from 0 to 127, each once within a row
Outputs:
- content_out: bfloat16 [2, 4096, 768], P('pipe', 'dp')
- query_out: bfloat16 [2, 512, 768], P('pipe', 'dp')
- grad_w_query: float32 [2, 768, 768], P('pipe')
- grad_b_query: float32 [2, 768], P('pipe')
- grad_w_key: float32 [2, 768, 768], P('pipe')
- grad_w_value: float32 [2, 768, 768], P('pipe')
- grad_b_value: float32 [2, 768], P('pipe')
- grad_w_out: float32 [2, 768, 768], P('pipe')
- grad_b_out: float32 [2, 768], P('pipe')
- grad_gain_attn: float32 [2, 768], P('pipe')
- grad_shift_attn: float32 [2, 768], P('pipe')
- grad_w_up: float32 [2, 768, 3072], P('pipe')
- grad_b_up: float32 [2, 3072], P('pipe')
- grad_w_down: float32 [2, 3072, 768], P('pipe')
- grad_b_down: float32 [2, 768], P('pipe')
- grad_gain_ffn: float32 [2, 768], P('pipe')
- grad_shift_ffn: float32 [2, 768], P('pipe')
- grad_rel_table: float32 [2, 32, 12], P('pipe')
Inputs may be any that keep to these rules, and one draw needn't show every extreme that they name: `doc_lengths`: each row lists the lengths of the 4 documents packed in order into one bucket; they sum to 128, and the longest is exactly 96. `position_order`: each row is a permutation of the 128 positions of one bucket; the positions named by its last 16 entries are the predicted ones.
All inputs are finite; a program needn't handle non-finite values.
Results may differ from a plain program's by a relative error of at most 0.03.
Values may be sent and summed in bfloat16 or wider, within the bound.
A program may use at most 256 MiB of HBM per device.

v0:
```python
import functools
import math
from typing import Any, NamedTuple

import jax
import jax.numpy as jnp
from jax import lax
from jax.experimental import pallas as pl
from jax.experimental.pallas import tpu as pltpu
from jax.sharding import PartitionSpec as P

MESH = pl.DeviceIdType.MESH
F32 = jnp.float32
BF16 = jnp.bfloat16
NORM_EPS = 1e-05
NEG_FILL = -1e30
THRESHOLDS = (12, 16, 23, 32, 46, 64, 91)
TILE = 256
LANES = 128
MATRICES = 6
VMEM_LIMIT = 60 * 2**20


def reduce_kernel(steps, lag, grads, smalls, out, smalls_out, core_in, own, final, from_y, end_b, end_a, mid_a, mid_b, rung_b, small_in, small_sum,
                  own_sem, core_sem, y_sem, eb_sem, ea_sem, ma_sem, mb_sem, rb_sem, fe_sem, fy_sem, fm_sem, fb_sem, sib_sem, small_sem, small_send, store_sem, send_sem):
    pipe, place = lax.axis_index("pipe"), lax.axis_index("dp")
    base = place // 16 * 16
    local = place % 16
    z, y, c = local // 4, local // 2 % 2, local % 2
    is_end = (z == 0) | (z == 3)
    is_mid = (z == 1) | (z == 2)
    inner = jnp.where(z == 0, 1, 2)
    outer = jnp.where(z == 1, 0, 3)
    mine = z + 1
    other = 4 - z

    def at(zz, yy, cc):
        return (pipe, base + zz * 4 + yy * 2 + cc)

    sibling, y_peer, z_in, z_out, z_mid = at(z, y, 1 - c), at(z, 1 - y, c), at(inner, y, c), at(outer, y, c), at(3 - z, y, c)
    partners = [(pipe, base + jnp.bitwise_xor(local, 1 << j)) for j in range(4)]

    barrier = pltpu.get_barrier_semaphore()

    def greet(device):
        pl.semaphore_signal(barrier, inc=1, device_id=device, device_id_type=MESH)

    for device in partners:
        greet(device)
    @pl.when(is_mid)
    def _():
        greet(z_mid)
        pl.semaphore_wait(barrier, 5)

    @pl.when(is_end)
    def _():
        pl.semaphore_wait(barrier, 4)

    def remote(src, dst, which, sem, device):
        return pltpu.make_async_remote_copy(src_ref=src, dst_ref=dst, send_sem=send_sem.at[which], recv_sem=sem, device_id=device, device_id_type=MESH)

    def recv(dst, sem):
        pltpu.make_async_copy(dst, dst, sem).wait()

    def small_copy(j):
        src = smalls if j == 0 else small_sum.at[j - 1]
        return pltpu.make_async_remote_copy(src_ref=src, dst_ref=small_in.at[j], send_sem=small_send.at[j], recv_sem=small_sem.at[j], device_id=partners[j], device_id_type=MESH)

    def small_step(j):
        cp = small_copy(j)
        cp.wait()
        held = smalls[...] if j == 0 else small_sum[j - 1]
        if j < 3:
            small_sum[j] = held + small_in[j]
            small_copy(j + 1).start()
        else:
            smalls_out[...] = held + small_in[j]

    small_copy(0).start()

    def s0(k):
        remote(grads.at[1 - c, k], core_in.at[k], 0, core_sem.at[k], sibling).start()
        pltpu.make_async_copy(grads.at[c, k], own.at[k], own_sem.at[k]).start()

    def s1(k):
        pltpu.make_async_copy(grads.at[c, k], own.at[k], own_sem.at[k]).wait()
        recv(core_in.at[k], core_sem.at[k])
        core_in[k] = (core_in[k].astype(F32) + own[k].astype(F32)).astype(BF16)
        remote(core_in.at[k, 1 - y], from_y.at[k], 1, y_sem.at[k], y_peer).start()

        @pl.when(is_end)
        def _():
            remote(core_in.at[k, pl.ds(2, 2)], end_b.at[k], 2, eb_sem.at[k], z_in).start()

    def s2(k):
        recv(from_y.at[k], y_sem.at[k])
        core_in[k, y] = (core_in[k, y].astype(F32) + from_y[k].astype(F32)).astype(BF16)

        @pl.when(is_end)
        def _():
            remote(core_in.at[k, y], end_a.at[k], 3, ea_sem.at[k], z_in).start()

        @pl.when(is_mid)
        def _():
            recv(end_b.at[k], eb_sem.at[k])
            core_in[k, pl.ds(2, 2)] = (core_in[k, pl.ds(2, 2)].astype(F32) + end_b[k].astype(F32)).astype(BF16)
            remote(core_in.at[k, other], mid_b.at[k], 4, mb_sem.at[k], z_mid).start()

    def s3(k):
        @pl.when(is_mid)
        def _():
            recv(end_a.at[k], ea_sem.at[k])
            core_in[k, y] = (core_in[k, y].astype(F32) + end_a[k].astype(F32)).astype(BF16)
            remote(core_in.at[k, y], mid_a.at[k], 5, ma_sem.at[k], z_mid).start()
            recv(mid_b.at[k], mb_sem.at[k])
            core_in[k, mine] = (core_in[k, mine].astype(F32) + mid_b[k].astype(F32)).astype(BF16)
            remote(core_in.at[k, mine], rung_b.at[k], 6, rb_sem.at[k], y_peer).start()

    def s4(k):
        @pl.when(is_mid)
        def _():
            recv(mid_a.at[k], ma_sem.at[k])
            final[c, k, y] = (core_in[k, y].astype(F32) + mid_a[k].astype(F32)).astype(BF16)
            remote(final.at[c, k, y], final.at[c, k, y], 7, fe_sem.at[k], z_out).start()
            remote(final.at[c, k, y], final.at[c, k, y], 8, fy_sem.at[k], y_peer).start()
            recv(rung_b.at[k], rb_sem.at[k])
            final[c, k, mine] = (core_in[k, mine].astype(F32) + rung_b[k].astype(F32)).astype(BF16)
            remote(final.at[c, k, mine], final.at[c, k, mine], 9, fm_sem.at[k], z_mid).start()

    def s5(k):
        @pl.when(is_end)
        def _():
            recv(final.at[c, k, y], fe_sem.at[k])
            remote(final.at[c, k, y], final.at[c, k, y], 8, fy_sem.at[k], y_peer).start()

        @pl.when(is_mid)
        def _():
            recv(final.at[c, k, other], fm_sem.at[k])
            remote(final.at[c, k, pl.ds(2, 2)], final.at[c, k, pl.ds(2, 2)], 10, fb_sem.at[k], z_out).start()

    def s6(k):
        recv(final.at[c, k, 1 - y], fy_sem.at[k])

        @pl.when(is_end)
        def _():
            recv(final.at[c, k, pl.ds(2, 2)], fb_sem.at[k])

        remote(final.at[c, k], final.at[c, k], 11, sib_sem.at[k], sibling).start()
        pltpu.make_async_copy(final.at[c, k], out.at[c, k], store_sem.at[0]).start()

    def s7(k):
        recv(final.at[1 - c, k], sib_sem.at[k])
        pltpu.make_async_copy(final.at[1 - c, k], out.at[1 - c, k], store_sem.at[1]).start()

    stages = (s0, s1, s2, s3, s4, s5, s6, s7)
    offsets = lag
    at_small = [min(steps - 1, 4 * (j + 1)) for j in range(4)]

    @pl.loop(0, steps + offsets[-1])
    def _(t):
        for stage, off in zip(stages, offsets):
            k = t - off

            @pl.when((k >= 0) & (k < steps))
            def _():
                stage(jnp.clip(k, 0, steps - 1))

        for j in range(4):
            @pl.when(t == 4 * (j + 1))
            def _():
                small_step(j)

    def sent(ref, which):
        pltpu.make_async_copy(ref, ref, send_sem.at[which]).wait()

    sent(core_in, 0)
    sent(from_y, 1)
    sent(final.at[0], 11)
    pltpu.make_async_copy(final.at[0], out.at[0], store_sem.at[0]).wait()
    pltpu.make_async_copy(final.at[0], out.at[0], store_sem.at[1]).wait()
    sent(from_y, 8)

    @pl.when(is_end)
    def _():
        sent(end_b, 2)
        sent(end_a, 3)

    @pl.when(is_mid)
    def _():
        for which in (4, 5, 6, 7, 9):
            sent(mid_a, which)
        sent(end_b, 10)


def reduce_call(grads, smalls, lag, cid=1):
    _, steps, _, rows, width = grads.shape
    block = (steps, rows, width)
    sems = [pltpu.SemaphoreType.DMA((steps,)) for _ in range(13)]
    return pl.pallas_call(
        functools.partial(reduce_kernel, steps, lag),
        out_shape=(jax.ShapeDtypeStruct(grads.shape, BF16), jax.ShapeDtypeStruct(smalls.shape, F32)),
        in_specs=[pl.BlockSpec(memory_space=pl.ANY), pl.BlockSpec(memory_space=pltpu.VMEM)],
        out_specs=(pl.BlockSpec(memory_space=pl.ANY), pl.BlockSpec(memory_space=pltpu.VMEM)),
        scratch_shapes=[
            pltpu.VMEM((steps, 4, rows, width), BF16),
            pltpu.VMEM((steps, 4, rows, width), BF16),
            pltpu.VMEM(grads.shape, BF16),
            pltpu.VMEM(block, BF16),
            pltpu.VMEM((steps, 2, rows, width), BF16),
            pltpu.VMEM(block, BF16),
            pltpu.VMEM(block, BF16),
            pltpu.VMEM(block, BF16),
            pltpu.VMEM(block, BF16),
            pltpu.VMEM((4,) + smalls.shape, F32),
            pltpu.VMEM((3,) + smalls.shape, F32),
            *sems,
            pltpu.SemaphoreType.DMA((4,)),
            pltpu.SemaphoreType.DMA((4,)),
            pltpu.SemaphoreType.DMA((2,)),
            pltpu.SemaphoreType.DMA((12,)),
        ],
        compiler_params=pltpu.CompilerParams(collective_id=cid, has_side_effects=True, vmem_limit_bytes=56 * 2**20),
    )(grads, smalls)


class Sizes(NamedTuple):
    micro: int
    seq: int
    query: int
    width: int
    heads: int
    hidden: int
    buckets: int

    @property
    def block(self):
        return self.seq + self.query

    @property
    def rows(self):
        return self.micro * self.block

    @property
    def pairs(self):
        return self.width // LANES


class Weights(NamedTuple):
    query: Any
    key: Any
    value: Any
    out: Any
    up: Any
    down: Any


class Vectors(NamedTuple):
    b_query: Any
    b_value: Any
    b_out: Any
    gain_attn: Any
    shift_attn: Any
    b_up: Any
    b_down: Any
    gain_ffn: Any
    shift_ffn: Any
    rel_table: Any
    lengths: Any
    order: Any


class State(NamedTuple):
    left: Any
    qkv: Any
    slope: Any
    probs: Any
    norm_attn: Any
    norm_ffn: Any
    spread_attn: Any
    spread_ffn: Any


def state_shapes(n):
    return State(
        ((n.rows, 3 * n.width + n.hidden), BF16),
        ((n.rows, 3 * n.width), BF16),
        ((n.rows, n.hidden), BF16),
        ((n.micro * n.pairs, 2 * n.block, n.seq), F32),
        ((n.rows, n.width), F32),
        ((n.rows, n.width), F32),
        ((n.rows, 1), F32),
        ((n.rows, 1), F32),
    )


def dot(a, b):
    return jnp.dot(a, b, preferred_element_type=F32)


def dot_nt(a, b, precision=None):
    return lax.dot_general(a, b, (((1,), (1,)), ((), ())), precision=precision, preferred_element_type=F32)


def dot_tn(a, b, precision=None):
    return lax.dot_general(a, b, (((0,), (0,)), ((), ())), precision=precision, preferred_element_type=F32)


def iota(shape, dim):
    return lax.broadcasted_iota(jnp.int32, shape, dim)


def cols(at, size=TILE):
    return pl.ds(pl.multiple_of(at * size, size), size)


def bucket_of(offset):
    distance = jnp.abs(offset)
    bucket = jnp.minimum(distance, 8) + jnp.where(offset < 0, 16, 0)
    for bound_at in THRESHOLDS:
        bucket = bucket + jnp.where(distance >= bound_at, 1, 0)
    return bucket


def place_buckets(n):
    shape = (n.buckets, 2 * n.seq)
    at = iota(shape, 1)
    offset = jnp.where(at < n.seq, -at, 2 * n.seq - at)
    return jnp.where(bucket_of(offset) == iota(shape, 0), 1.0, 0.0)


def to_column(row, n):
    shape = (n.seq, n.seq)
    return jnp.sum(jnp.where(iota(shape, 0) == iota(shape, 1), row, 0.0), axis=1, keepdims=True)


def picked(order_col, n, place):
    return order_col[n.seq - n.query :] == place.astype(F32)


def bias_and_mask(n, v, bias):
    seq, query = n.seq, n.query
    base = dot_tn(v.rel_table[0], place_buckets(n), lax.Precision.HIGHEST)
    square = (seq, seq)
    row_at, col_at = iota(square, 0).astype(F32), iota(square, 1).astype(F32)
    visible_from = float(seq - query)
    content_sees, query_sees, chosen = [], [], []
    for b in range(n.micro):
        order_row = v.order[b : b + 1, :].astype(F32)
        order_col = to_column(order_row, n)
        rank_row = jnp.sum(jnp.where(order_col == col_at, row_at, 0.0), axis=0, keepdims=True)
        rank_col = to_column(rank_row, n)
        ends, total = [], jnp.int32(0)
        for d in range(v.lengths.shape[1]):
            total = total + v.lengths[b, d]
            ends.append(total)

        def doc_of(at):
            found = jnp.zeros(at.shape, F32)
            for end in ends:
                found = found + jnp.where(at >= end.astype(F32), 1.0, 0.0)
            return found

        doc_row = doc_of(iota((1, seq), 1).astype(F32))
        doc_col = doc_of(iota((seq, 1), 0).astype(F32))
        unmasked = rank_row < visible_from
        content_sees.append((doc_col == doc_row) & (unmasked | (rank_row <= rank_col)))
        at_place = picked(order_col, n, iota((query, seq), 1))
        place = order_col[seq - query :]
        rank = visible_from + iota((query, 1), 0).astype(F32)
        query_sees.append((doc_of(place) == doc_row) & (unmasked | (rank_row < rank) | at_place))
        chosen.append(jnp.where(at_place, 1.0, 0.0).astype(BF16))
    for h in range(n.heads):
        spread = jnp.broadcast_to(base[h : h + 1, :], (seq, 2 * seq))
        table = pltpu.roll(spread, 0, 1, stride=1, stride_axis=0)[:, :seq]
        high = table.astype(BF16)
        rest = table - high.astype(F32)
        middle = rest.astype(BF16)
        low = (rest - middle.astype(F32)).astype(BF16)
        for b in range(n.micro):
            of_query = dot(chosen[b], high) + dot(chosen[b], middle) + dot(chosen[b], low)
            start = (h % 2) * n.block
            bias[b, h // 2, start : start + seq, :] = jnp.where(content_sees[b], table, NEG_FILL)
            bias[b, h // 2, start + seq : start + n.block, :] = jnp.where(query_sees[b], of_query, NEG_FILL)


def half_masks():
    at = iota((1, LANES), 1)
    return jnp.where(at < LANES // 2, 1.0, 0.0).astype(BF16), jnp.where(at < LANES // 2, 0.0, 1.0).astype(BF16)


def both_heads(values):
    first, second = half_masks()
    return jnp.concatenate([values * first, values * second], axis=0)


def side_by_side(stacked):
    half = stacked.shape[0] // 2
    return jnp.concatenate([stacked[:half], stacked[half:]], axis=1)


def norm_rows(n, summed, spread_ref, gain, shift, write):
    step = n.block // 3

    @pl.loop(0, n.rows // step)
    def _(i):
        rows = pl.ds(pl.multiple_of(i * step, step), step)
        r = summed[rows, :]
        centered = r - jnp.mean(r, axis=1, keepdims=True)
        spread = lax.rsqrt(jnp.mean(centered * centered, axis=1, keepdims=True) + NORM_EPS)
        normed = centered * spread
        summed[rows, :] = normed
        spread_ref[rows, :] = spread
        write(rows, (normed * gain + shift).astype(BF16))


def norm_back(n, grad_of, normed_ref, spread_ref, gain, write):
    step = n.block // 3

    def body(i, sums):
        rows = pl.ds(pl.multiple_of(i * step, step), step)
        grad = grad_of(rows)
        normed = normed_ref[rows, :]
        scaled = grad * gain
        inner = jnp.mean(scaled * normed, axis=1, keepdims=True)
        back = spread_ref[rows, :] * (scaled - jnp.mean(scaled, axis=1, keepdims=True) - normed * inner)
        write(rows, back)
        low = back.astype(BF16).astype(F32)
        return (
            sums[0] + jnp.sum(grad * normed, axis=0, keepdims=True),
            sums[1] + jnp.sum(grad, axis=0, keepdims=True),
            sums[2] + jnp.sum(low, axis=0, keepdims=True),
        )

    zero = jnp.zeros((1, n.width), F32)
    return lax.fori_loop(0, n.rows // step, body, (zero, zero, zero))


def forward(n, ready, w, v, bias, s, y):
    width, tiles = n.width, n.width // TILE
    left_o, left_h, left_u = tiles, 2 * tiles, 3 * tiles
    for i, matrix in enumerate((w.query, w.key, w.value)):
        ready(i)

        @pl.loop(0, tiles)
        def _(t):
            product = dot(s.left[:, :width], matrix[:, cols(t)])
            if i == 0:
                product = product + v.b_query[:, cols(t)]
            if i == 2:
                product = product + v.b_value[:, cols(t)]
            s.qkv[:, cols(i * tiles + t)] = product.astype(BF16)

    factor = (LANES // 2) ** -0.5

    @pl.loop(0, n.micro * n.pairs)
    def _(it):
        b, pair = it // n.pairs, it % n.pairs
        rows = pl.ds(pl.multiple_of(b * n.block, 16), n.block)
        keys = pl.ds(pl.multiple_of(b * n.block, 16), n.seq)
        q = both_heads(s.qkv[rows, cols(pair, LANES)])
        k = s.qkv[keys, cols(n.pairs + pair, LANES)]
        val = both_heads(s.qkv[keys, cols(2 * n.pairs + pair, LANES)])
        scores = dot_nt(q, k) * factor + bias[b, pair]
        powers = jnp.exp(scores - jnp.max(scores, axis=1, keepdims=True))
        probs = powers / jnp.sum(powers, axis=1, keepdims=True)
        s.probs[it] = probs
        mixed = dot(side_by_side(probs.astype(BF16)), val)
        s.left[rows, cols(n.pairs + pair, LANES)] = mixed.astype(BF16)

    ready(3)

    @pl.loop(0, tiles)
    def _(t):
        product = dot(s.left[:, width : 2 * width], w.out[:, cols(t)])
        s.norm_attn[:, cols(t)] = s.left[:, cols(t)].astype(F32) + product + v.b_out[:, cols(t)]

    def keep_h1(rows, value):
        s.left[rows, 2 * width : 3 * width] = value

    norm_rows(n, s.norm_attn, s.spread_attn, v.gain_attn[...], v.shift_attn[...], keep_h1)
    ready(4)

    @pl.loop(0, n.hidden // TILE)
    def _(t):
        z = dot(s.left[:, 2 * width : 3 * width], w.up[:, cols(t)]) + v.b_up[:, cols(t)]
        c = (2 / math.pi) ** 0.5
        square = z * z
        bend = jnp.tanh(c * z * (1.0 + 0.044715 * square))
        half = 0.5 * (1.0 + bend)
        s.left[:, cols(left_u + t)] = (z * half).astype(BF16)
        s.slope[:, cols(t)] = (half + 0.5 * c * z * (1.0 - bend * bend) * (1.0 + 0.134145 * square)).astype(BF16)

    ready(5)

    @pl.loop(0, tiles)
    def _(t):
        product = dot(s.left[:, 3 * width :], w.down[:, cols(t)])
        s.norm_ffn[:, cols(t)] = s.left[:, cols(left_h + t)].astype(F32) + product + v.b_down[:, cols(t)]

    def keep_y(rows, value):
        y[rows, :] = value

    norm_rows(n, s.norm_ffn, s.spread_ffn, v.gain_ffn[...], v.shift_ffn[...], keep_y)


def backward(n, ready, w, v, s, dy, right, smalls, resid, table_sum, dx):
    width, tiles = n.width, n.width // TILE
    hidden_tiles = n.hidden // TILE
    at_da, at_dz = 3 * tiles, 4 * tiles
    at_df = at_dz + hidden_tiles
    df_cols = slice(at_df * TILE, at_df * TILE + width)
    da_cols = slice(3 * width, 4 * width)

    def keep_df(rows, value):
        resid[rows, :] = value
        right[rows, df_cols] = value.astype(BF16)

    gain, shift, low = norm_back(n, lambda rows: dy[rows, :].astype(F32), s.norm_ffn, s.spread_ffn, v.gain_ffn[...], keep_df)
    smalls[10:11, :], smalls[11:12, :], smalls[9:10, :] = gain, shift, low
    ready(5)

    @pl.loop(0, n.hidden // width)
    def _(group):
        @pl.loop(0, tiles)
        def _(inside):
            t = group * tiles + inside
            spread = dot_nt(right[:, df_cols], w.down[cols(t), :])
            dz = (spread * s.slope[:, cols(t)].astype(F32)).astype(BF16)
            right[:, cols(at_dz + t)] = dz
            smalls[pl.ds(5 + group, 1), cols(inside)] = jnp.sum(dz.astype(F32), axis=0, keepdims=True)

    ready(4)

    @pl.loop(0, tiles)
    def _(t):
        spread = dot_nt(right[:, at_dz * TILE : at_df * TILE], w.up[cols(t), :])
        dy[:, cols(t)] = (spread + resid[:, cols(t)]).astype(BF16)

    def keep_da(rows, value):
        resid[rows, :] = value
        right[rows, da_cols] = value.astype(BF16)

    gain, shift, low = norm_back(n, lambda rows: dy[rows, :].astype(F32), s.norm_attn, s.spread_attn, v.gain_attn[...], keep_da)
    smalls[3:4, :], smalls[4:5, :], smalls[2:3, :] = gain, shift, low
    ready(3)

    @pl.loop(0, tiles)
    def _(t):
        dy[:, cols(t)] = dot_nt(right[:, da_cols], w.out[cols(t), :]).astype(BF16)

    factor = (LANES // 2) ** -0.5
    table_sum[...] = jnp.zeros(table_sum.shape, F32)
    for b in range(n.micro):
        order_col = to_column(v.order[b : b + 1, :].astype(F32), n)
        square = (n.seq, n.seq)
        same = jnp.where(iota(square, 0) + iota(square, 1) == n.seq - 1, 1.0, 0.0)
        predicted = picked(order_col, n, n.seq - 1 - iota((n.query, n.seq), 1))
        chosen = jnp.concatenate([same, jnp.where(predicted, 1.0, 0.0)], axis=0).astype(BF16)

        @pl.loop(0, n.pairs)
        def _(pair):
            it = b * n.pairs + pair
            rows = slice(b * n.block, (b + 1) * n.block)
            keys = slice(b * n.block, b * n.block + n.seq)
            rest = slice(b * n.block + n.seq, (b + 1) * n.block)
            grad = both_heads(dy[rows, cols(pair, LANES)])
            q = both_heads(s.qkv[rows, cols(pair, LANES)])
            k = both_heads(s.qkv[keys, cols(n.pairs + pair, LANES)])
            val = s.qkv[keys, cols(2 * n.pairs + pair, LANES)]
            probs = s.probs[it]
            grad_probs = dot_nt(grad, val)
            inner = jnp.sum(probs * grad_probs, axis=1, keepdims=True)
            grad_scores = (probs * (grad_probs - inner)).astype(BF16)
            right[rows, cols(pair, LANES)] = (dot(side_by_side(grad_scores), k) * factor).astype(BF16)
            right[keys, cols(n.pairs + pair, LANES)] = (dot_tn(grad_scores, q) * factor).astype(BF16)
            right[keys, cols(2 * n.pairs + pair, LANES)] = dot_tn(probs.astype(BF16), grad).astype(BF16)
            none = jnp.zeros((n.query, LANES), BF16)
            right[rest, cols(n.pairs + pair, LANES)] = none
            right[rest, cols(2 * n.pairs + pair, LANES)] = none
            for half in range(2):
                of_head = grad_scores[half * n.block : (half + 1) * n.block]
                table_sum[2 * pair + half] += dot_tn(chosen, of_head)

    smalls[0:1, :] = jnp.sum(right[:, :width].astype(F32), axis=0, keepdims=True)
    smalls[1:2, :] = jnp.sum(right[:, 2 * width : 3 * width].astype(F32), axis=0, keepdims=True)
    by_place = []
    for h in range(n.heads):
        wide = jnp.concatenate([table_sum[h], jnp.zeros((n.seq, n.seq), F32)], axis=1)
        turned = pltpu.roll(wide, n.seq + 1, 1, stride=1, stride_axis=0)
        by_place.append(jnp.sum(turned, axis=0, keepdims=True))
    by_place = jnp.concatenate(by_place, axis=0)
    smalls[12 : 12 + n.heads, : n.buckets] = dot_nt(by_place, place_buckets(n), lax.Precision.HIGHEST)
    ready(0)
    ready(1)
    ready(2)

    @pl.loop(0, tiles)
    def _(t):
        total = resid[:, cols(t)]
        for i, matrix in enumerate((w.query, w.key, w.value)):
            total = total + dot_nt(right[:, i * width : (i + 1) * width], matrix[cols(t), :])
        dx[:, cols(t)] = total.astype(BF16)


def weight_grads(n, left, right, packed, write):
    width, tiles = n.width, n.width // TILE
    up_groups = n.hidden // width

    def tile(at, left_tile, right_group):
        lhs = left[:, cols(left_tile)]
        rhs = right[:, pl.ds(pl.multiple_of(right_group * width, width), width)]
        packed[cols(at), :] = dot_tn(lhs, rhs).astype(BF16)
        write(at)

    @pl.loop(0, 3 * tiles)
    def _(i):
        tile(i, i % tiles, i // tiles)

    @pl.loop(0, tiles)
    def _(i):
        tile(3 * tiles + i, tiles + i, 3)

    @pl.loop(0, up_groups * tiles)
    def _(i):
        tile(4 * tiles + i, 2 * tiles + i % tiles, 4 + i // tiles)

    @pl.loop(0, n.hidden // TILE)
    def _(i):
        tile((4 + up_groups) * tiles + i, 3 * tiles + i, 4 + up_groups)


def copies_of(pairs, sems):
    return [pltpu.make_async_copy(src, dst, sems.at[i]) for i, (src, dst) in enumerate(pairs)]


def rows_in(n, content, query, wide, sems, back=False):
    pairs = []
    for b in range(n.micro):
        pairs.append((content.at[0, pl.ds(b * n.seq, n.seq)], wide.at[pl.ds(b * n.block, n.seq)]))
        pairs.append((query.at[0, pl.ds(b * n.query, n.query)], wide.at[pl.ds(b * n.block + n.seq, n.query)]))
    if back:
        pairs = [(dst, src) for src, dst in pairs]
    return copies_of(pairs, sems)


def once(copies):
    done = set()

    def ready(i):
        if i not in done:
            done.add(i)
            copies[i].wait()

    return ready


def first_kernel(n, *refs):
    content, query, *refs = refs
    w_hbm, refs = Weights(*refs[:6]), refs[6:]
    v, refs = Vectors(*refs[:12]), refs[12:]
    y, refs = refs[0], refs[1:]
    s_out, refs = State(*refs[:8]), refs[8:]
    w, refs = Weights(*refs[:6]), refs[6:]
    s, refs = State(*refs[:8]), refs[8:]
    bias, w_sem, row_sem, s_sem = refs

    @pl.when(lax.axis_index("pipe") == 0)
    def _():
        rows = rows_in(n, content, query, s.left.at[:, pl.ds(0, n.width)], row_sem)
        for cp in rows:
            cp.start()
        weights = copies_of([(a.at[0], b) for a, b in zip(w_hbm, w)], w_sem)
        for cp in weights:
            cp.start()
        bias_and_mask(n, v, bias)
        for cp in rows:
            cp.wait()
        forward(n, once(weights), w, v, bias, s, y)
        kept = copies_of(list(zip(s, s_out)), s_sem)
        for cp in kept:
            cp.start()
        for cp in kept:
            cp.wait()


def second_kernel(n, *refs):
    arrived, content, query, *refs = refs
    w_hbm, refs = Weights(*refs[:6]), refs[6:]
    v, refs = Vectors(*refs[:12]), refs[12:]
    y, dx, left_out, right_out, smalls, *refs = refs
    w, refs = Weights(*refs[:6]), refs[6:]
    s, refs = State(*refs[:8]), refs[8:]
    bias, dy, right, resid, table_sum, w_sem, row_sem, s_sem = refs

    @pl.when(lax.axis_index("pipe") == 1)
    def _():
        rows = rows_in(n, content, query, dy, row_sem)
        mine = pltpu.make_async_copy(arrived, s.left.at[:, pl.ds(0, n.width)], s_sem.at[0])
        mine.start()
        weights = copies_of([(a.at[0], b) for a, b in zip(w_hbm, w)], w_sem)
        for cp in weights:
            cp.start()
        for cp in rows:
            cp.start()
        bias_and_mask(n, v, bias)
        mine.wait()
        ready = once(weights)
        forward(n, ready, w, v, bias, s, y)
        for cp in rows:
            cp.wait()
        kept = pltpu.make_async_copy(s.left, left_out, s_sem.at[0])
        kept.start()
        backward(n, ready, w, v, s, dy, right, smalls, resid, table_sum, dx)
        also = pltpu.make_async_copy(right, right_out, s_sem.at[1])
        also.start()
        kept.wait()
        also.wait()


def third_kernel(n, *refs):
    arrived, y, left_in, right_in, smalls_in, *refs = refs
    s_in, refs = State(*refs[:8]), refs[8:]
    w_hbm, refs = Weights(*refs[:6]), refs[6:]
    v, refs = Vectors(*refs[:12]), refs[12:]
    content_out, query_out, packed_out, smalls, *refs = refs
    w, refs = Weights(*refs[:6]), refs[6:]
    s, refs = State(*refs[:8]), refs[8:]
    dy, dx, right, resid, table_sum, packed, w_sem, row_sem, s_sem, out_sem = refs
    pipe = lax.axis_index("pipe")

    @pl.when(pipe == 0)
    def _():
        mine = pltpu.make_async_copy(arrived, dy, row_sem.at[0])
        mine.start()
        kept = copies_of(list(zip(s_in, s)), s_sem)
        for cp in reversed(kept):
            cp.start()
        weights = copies_of([(a.at[0], b) for a, b in zip(w_hbm, w)], w_sem)
        for cp in reversed(weights):
            cp.start()
        mine.wait()
        for cp in kept:
            cp.wait()
        backward(n, once(weights), w, v, s, dy, right, smalls, resid, table_sum, dx)

    @pl.when(pipe == 1)
    def _():
        kept = copies_of([(left_in, s.left), (right_in, right), (y, dx)], s_sem)
        for cp in kept:
            cp.start()
        smalls[...] = smalls_in[...]
        for cp in kept:
            cp.wait()

    outs = rows_in(n, content_out, query_out, dx, row_sem, back=True)
    for cp in outs:
        cp.start()

    def store(at):
        return pltpu.make_async_copy(packed.at[cols(at)], packed_out.at[cols(at)], out_sem)

    weight_grads(n, s.left, right, packed, lambda at: store(at).start())
    for cp in outs:
        cp.wait()
    pltpu.make_async_copy(packed, packed_out, out_sem).wait()


def any_specs(count):
    return [pl.BlockSpec(memory_space=pl.ANY)] * count


def vector_specs():
    vmem = pl.BlockSpec(memory_space=pltpu.VMEM)
    return [vmem] * 10 + [pl.BlockSpec(memory_space=pltpu.SMEM), vmem]


def shaped(shape, dtype=BF16):
    return jax.ShapeDtypeStruct(shape, dtype)


def run_layers(n, content, query, w, v):
    rows, width = n.rows, n.width
    act = shaped((rows, width))
    packed = ((4 * width + 2 * n.hidden), width)
    right = (rows, 5 * width + n.hidden)
    small_shape = (24, width)
    w_scratch = [pltpu.VMEM(m.shape[1:], BF16) for m in w]
    s_shapes = state_shapes(n)
    s_scratch = [pltpu.VMEM(shape, dtype) for shape, dtype in s_shapes]
    bias = pltpu.VMEM((n.micro, n.pairs, 2 * n.block, n.seq), F32)
    dma = pltpu.SemaphoreType.DMA
    params = pltpu.CompilerParams(vmem_limit_bytes=VMEM_LIMIT)
    vmem, anywhere = pl.BlockSpec(memory_space=pltpu.VMEM), pl.BlockSpec(memory_space=pl.ANY)
    y0, *kept = pl.pallas_call(
        functools.partial(first_kernel, n),
        out_shape=[act] + [shaped(*s) for s in s_shapes],
        in_specs=any_specs(8) + vector_specs(),
        out_specs=[vmem] + any_specs(8),
        scratch_shapes=w_scratch + s_scratch + [bias, dma((6,)), dma((2 * n.micro,)), dma((8,))],
        compiler_params=params,
    )(content, query, *w, *v)
    arrived = lax.ppermute(y0, "pipe", [(0, 1)])
    y1, dx1, left1, right1, smalls1 = pl.pallas_call(
        functools.partial(second_kernel, n),
        out_shape=[act, act, shaped(s_shapes.left[0]), shaped(right), shaped(small_shape, F32)],
        in_specs=any_specs(9) + vector_specs(),
        out_specs=[vmem, vmem, anywhere, anywhere, vmem],
        scratch_shapes=w_scratch
        + s_scratch
        + [bias, pltpu.VMEM((rows, width), BF16), pltpu.VMEM(right, BF16), pltpu.VMEM((rows, width), F32), pltpu.VMEM((n.heads, n.seq, n.seq), F32)]
        + [dma((6,)), dma((2 * n.micro,)), dma((2,))],
        compiler_params=params,
    )(arrived, content, query, *w, *v)
    returned = lax.ppermute(dx1, "pipe", [(1, 0)])
    return pl.pallas_call(
        functools.partial(third_kernel, n),
        out_shape=[shaped(content.shape), shaped(query.shape), shaped(packed), shaped(small_shape, F32)],
        in_specs=any_specs(4) + [vmem] + any_specs(14) + vector_specs(),
        out_specs=any_specs(3) + [vmem],
        scratch_shapes=w_scratch
        + s_scratch
        + [pltpu.VMEM((rows, width), BF16), pltpu.VMEM((rows, width), BF16), pltpu.VMEM(right, BF16), pltpu.VMEM((rows, width), F32), pltpu.VMEM((n.heads, n.seq, n.seq), F32), pltpu.VMEM(packed, BF16)]
        + [dma((6,)), dma((2 * n.micro,)), dma((8,)), dma],
        compiler_params=params,
    )(returned, y1, left1, right1, smalls1, *kept, *w, *v)


def unpack(n, packed, smalls):
    width, heads = n.width, n.heads
    parts = packed.reshape(-1, width, width)
    groups = n.hidden // width
    whole = [parts[i].astype(F32)[None] for i in range(4)]
    whole.append(jnp.concatenate([parts[4 + i] for i in range(groups)], axis=1).astype(F32)[None])
    whole.append(packed[(4 + groups) * width :].astype(F32)[None])
    vectors = [smalls[i : i + 1] for i in range(5)]
    vectors.append(smalls[5 : 5 + groups].reshape(1, n.hidden))
    vectors += [smalls[i : i + 1] for i in range(5 + groups, 8 + groups)]
    vectors.append(smalls[12 : 12 + heads, : n.buckets].T[None])
    return whole, vectors


def all_sums(packed, smalls):
    steps_of = 8 * 16
    size = lax.axis_size("dp")
    if size % 16 or packed.shape[0] % steps_of:
        return lax.psum(packed.astype(F32), "dp"), lax.psum(smalls, "dp")
    lag = (0, 2, 4, 6, 8, 10, 12, 14)
    width = packed.shape[1]
    final, smalls = reduce_call(packed.reshape(2, packed.shape[0] // steps_of, 4, 16, width), smalls, lag)
    if size > 16:
        groups = [[b * 16 + i for b in range(size // 16)] for i in range(16)]
        final = lax.psum(final.astype(F32), "dp", axis_index_groups=groups)
        smalls = lax.psum(smalls, "dp", axis_index_groups=groups)
    return final.reshape(packed.shape), smalls


def on_device(content_ends, query_ends, w_query, b_query, w_key, w_value, b_value, w_out, b_out, gain_attn, shift_attn, w_up, b_up, w_down, b_down, gain_ffn, shift_ffn, rel_table, doc_lengths, position_order):
    micro, seq = position_order.shape
    n = Sizes(micro, seq, query_ends.shape[1] // micro, content_ends.shape[2], rel_table.shape[2], w_up.shape[2], rel_table.shape[1])
    w = Weights(w_query, w_key, w_value, w_out, w_up, w_down)
    v = Vectors(b_query, b_value, b_out, gain_attn, shift_attn, b_up, b_down, gain_ffn, shift_ffn, rel_table, doc_lengths, position_order)
    content_out, query_out, packed, smalls = run_layers(n, content_ends, query_ends, w, v)
    packed, smalls = all_sums(packed, smalls)
    g, d = unpack(n, packed, smalls)
    return content_out, query_out, g[0], d[0], g[1], g[2], d[1], g[3], d[2], d[3], d[4], g[4], d[5], g[5], d[6], d[7], d[8], d[9]


def solution(mesh):
    rows, matrix, vector, buckets = P("pipe", "dp", None), P("pipe", None, None), P("pipe", None), P("dp", None)
    grads = (matrix, vector, matrix, matrix, vector, matrix, vector, vector, vector, matrix, vector, matrix, vector, vector, vector, matrix)
    return jax.shard_map(on_device, mesh=mesh, in_specs=(rows, rows, *grads, buckets, buckets), out_specs=(rows, rows, *grads), check_vma=False)
```

profile of v0, /device:TPU:0, one launch (start us, length us, event | category | flops | bytes accessed | tf_op | source)
XLA Modules:
  0.0 316.4 jit_solution(874642237286171956)
XLA Ops:
  0.7 1.4 copy.38.refs_17_.refs_18_.refs_28_
  2.0 28.4 %shard_map.331 = (bf16[288,768]{1,0:T(8,128)(2,1)}, bf16[288,5376]{1,0:T(8,128)(2,1)}, bf16[288,2304]{1,0:T(8,128)(2,1)}, bf16[288,3072]{1,0:T(8,128)(2,1)}, f32...) custom-call(bf16[1,256,768]{2,1,0:T(8,128)(2,1)} %refs_1_.3, ...), custom_call_target="tpu_custom_call" | custom-call | tf_op jit(solution)/shard_map/pallas_call | solution.py:794
  30.4 1.3 collective-permute-start
  31.7 10.6 %collective-permute-done.refs_0_ = bf16[288,768]{1,0:T(8,128)(2,1)S(1)} collective-permute-done((bf16[288,768]{1,0:T(8,128)(2,1)}, bf16[288,768]{1,0:T(8,128)(2,1)S(1)}, u32[]{:S(2)}, u32[]{:S(2)}) %collective-permute-start) | collective-permute-done | bytes 442400 | tf_op jit(solution)/shard_map/ppermute | solution.py:802
  42.3 0.0 copy-start.2
  42.3 0.8 copy-done.2
  43.1 1.9 shard_map.332
  45.0 1.3 collective-permute-start.1
  46.3 55.5 %collective-permute-done.1.refs_0_ = bf16[288,768]{1,0:T(8,128)(2,1)S(1)} collective-permute-done((bf16[288,768]{1,0:T(8,128)(2,1)}, bf16[288,768]{1,0:T(8,128)(2,1)S(1)}, u32[]{:S(2)}, u32[]{:S(2)}) %collective-permute-start.1) | collective-permute-done | bytes 442400 | tf_op jit(solution)/shard_map/ppermute | solution.py:814
  101.7 0.0 copy-start.1
  101.7 0.8 copy-done.1
  102.5 43.5 %shard_map.333 = (bf16[1,256,768]{2,1,0:T(8,128)(2,1)}, bf16[1,32,768]{2,1,0:T(8,128)(2,1)}, bf16[9216,768]{1,0:T(8,128)(2,1)}, f32[24,768]{1,0:T(8,128)}) custom-call(bf16[288,768]{1,0:T(8,128)(2,1)} %copy-done.1, bf16[288,768]{1,0:T(8,128)(2,1)} %get-tuple-element.40.refs_1_, bf16[288,5376]{1,0:T(8,128)(2,1)} %get-tuple-element.41.refs_2_, ...), custom_call_target="tpu_custom_call" | custom-call | tf_op jit(solution)/shard_map/pallas_call | solution.py:815
  146.0 148.1 %shard_map.334 = (bf16[2,72,4,16,768]{4,3,2,1,0:T(8,128)(2,1)}, f32[24,768]{1,0:T(8,128)}) custom-call(bf16[2,72,4,16,768]{4,3,2,1,0:T(8,128)(2,1)} %bitcast.16, f32[24,768]{1,0:T(8,128)} %get-tuple-element.55.smalls), custom_call_target="tpu_custom_call" | custom-call | tf_op jit(solution)/shard_map/pallas_call | solution.py:199
  294.2 0.7 slice_bitcast_fusion.2
  294.9 0.8 slice_bitcast_fusion.1
  295.7 1.5 fusion.2
  297.2 0.6 copy.41
  297.8 0.6 copy.42
  298.4 0.0 copy-start
  298.4 8.0 %fusion = f32[1,3072,768]{2,1,0:T(8,128)} fusion(bf16[9216,768]{1,0:T(8,128)(2,1)} %bitcast.17), kind=kLoop, calls=%fused_computation.1 | loop fusion | flops 2359296 | bytes 14155776 | tf_op jit(solution)/shard_map/broadcast_in_dim | solution.py:834
  306.4 1.8 copy-done
  308.3 3.8 %fusion.1 = (bf16[1,768,768]{2,1,0:T(8,128)(2,1)S(1)}, bf16[1,768,768]{2,1,0:T(8,128)(2,1)S(1)}, bf16[1,768,768]{2,1,0:T(8,128)(2,1)S(1)}, bf16[1,768,768]{2,1,0...) fusion(bf16[12,768,768]{2,1,0:T(8,128)(2,1)S(1)} %bitcast.18), kind=kLoop, calls=%fused_computation.9 | loop fusion | flops 2359296 | bytes 23592960 | tf_op jit(solution)/shard_map/slice | solution.py:833
  312.0 4.3 %maximum_convert_fusion = f32[1,768,3072]{2,1,0:T(8,128)} fusion(bf16[1,768,768]{2,1,0:T(8,128)(2,1)S(1)} %get-tuple-element.77, bf16[1,768,768]{2,1,0:T(8,128)(2,1)S(1)} %get-tuple-element.78, bf16[1,768,768]{2,1,0:T(8,128)(2,1)S(1)} %get-tuple-element.79, bf16[1,768,768]{2,1,0:T(8,128)(2,1)S(1)} %get-tuple-element.76), kind=kLoop, calls=%fused_computation.2 | loop fusion | flops 18874368 | bytes 14155776 | tf_op jit(solution)/shard_map/convert_element_type | solution.py:833
Async XLA Ops:
  30.4 11.9 %collective-permute-start = (bf16[288,768]{1,0:T(8,128)(2,1)}, bf16[288,768]{1,0:T(8,128)(2,1)S(1)}, u32[]{:S(2)}, u32[]{:S(2)}) collective-permute-start(bf16[288,768]{1,0:T(8,128)(2,1)} %get-tuple-element.38), channel_id=1, source_target_pairs={{0,16},{1,17},{2,18},{3,19},{4,20},{5,21},{6,22},{7,23},{8,24},{9,... | collective-permute-start | bytes 1327112 | tf_op jit(solution)/shard_map/ppermute | solution.py:802
  42.3 0.8 copy-start.2
  45.0 56.8 %collective-permute-start.1 = (bf16[288,768]{1,0:T(8,128)(2,1)}, bf16[288,768]{1,0:T(8,128)(2,1)S(1)}, u32[]{:S(2)}, u32[]{:S(2)}) collective-permute-start(bf16[288,768]{1,0:T(8,128)(2,1)} %get-tuple-element.39), channel_id=1, source_target_pairs={{16,0},{17,1},{18,2},{19,3},{20,4},{21,5},{22,6},{23,7},{24,8},{25... | collective-permute-start | bytes 1327112 | tf_op jit(solution)/shard_map/ppermute | solution.py:814
  101.7 0.8 copy-start.1
  298.4 9.8 %copy-start = (bf16[2,72,4,16,768]{4,3,2,1,0:T(8,128)(2,1)S(1)}, bf16[2,72,4,16,768]{4,3,2,1,0:T(8,128)(2,1)}, u32[]{:S(2)}) copy-start(bf16[2,72,4,16,768]{4,3,2,1,0:T(8,128)(2,1)} %get-tuple-element.56) | copy-start | bytes 42467332
where the time goes:
time: 318 us; the launch traced here: 316 us
  Pallas kernels  222 us (70%)
  waiting for transfers between devices  66 us (21%)
  other arithmetic  16.1 us (5%)
  local copies, waits for them, and re-layouts  9 us (3%)
    pallas_call x1, Pallas kernels, reduce_call(): pl.pallas_call(functools.partial(reduce_kernel, steps, lag), out_shape=(j...  148 us
    ppermute x1, waiting for transfers between devices, run_layers(): returned = lax.ppermute(dx1, 'pipe', [(1, 0)])  55.5 us
    pallas_call x1, Pallas kernels, run_layers(): pl.pallas_call(functools.partial(third_kernel, n), out_shape=[shaped(cont...  43.5 us
    pallas_call x1, Pallas kernels, run_layers(): pl.pallas_call(functools.partial(first_kernel, n), out_shape=[act] + [sha...  28.4 us
    ppermute x1, waiting for transfers between devices, run_layers(): arrived = lax.ppermute(y0, 'pipe', [(0, 1)])  10.6 us
    broadcast_in_dim x1, other arithmetic, unpack(): whole.append(packed[(4 + groups) * width:].astype(F32)[None])  8.01 us
    unnamed x10, local copies, waits for them, and re-layouts  6.76 us
  transfers between devices with their start and end apart: 2, of which 2 were waited for; matrix products, arithmetic and copies ran while one was open for 0% of the time, Pallas kernels for 0%

commit v1 on v0

v1 whole, which is shorter than its diff:
```python
import functools
import math
from typing import Any, NamedTuple

import jax
import jax.numpy as jnp
from jax import lax
from jax.experimental import pallas as pl
from jax.experimental.pallas import tpu as pltpu
from jax.sharding import PartitionSpec as P

MESH = pl.DeviceIdType.MESH
F32 = jnp.float32
BF16 = jnp.bfloat16
NORM_EPS = 1e-05
NEG_FILL = -1e30
THRESHOLDS = (12, 16, 23, 32, 46, 64, 91)
TILE = 256
LANES = 128
UNROLL = 3
EARLY = 3
LAG = 2
CHUNK = 16
VMEM_LIMIT = 63 * 2**20


class Sizes(NamedTuple):
    micro: int
    seq: int
    query: int
    width: int
    heads: int
    hidden: int
    buckets: int

    @property
    def block(self):
        return self.seq + self.query

    @property
    def rows(self):
        return self.micro * self.block

    @property
    def pairs(self):
        return self.width // LANES


class Weights(NamedTuple):
    query: Any
    key: Any
    value: Any
    out: Any
    up: Any
    down: Any


class Vectors(NamedTuple):
    b_query: Any
    b_value: Any
    b_out: Any
    gain_attn: Any
    shift_attn: Any
    b_up: Any
    b_down: Any
    gain_ffn: Any
    shift_ffn: Any
    rel_table: Any
    lengths: Any
    order: Any


class State(NamedTuple):
    left: Any
    qkv: Any
    slope: Any
    probs: Any
    norm_attn: Any
    norm_ffn: Any
    spread_attn: Any
    spread_ffn: Any


def state_shapes(n):
    return State(
        ((n.rows, 3 * n.width + n.hidden), BF16),
        ((n.rows, 3 * n.width), BF16),
        ((n.rows, n.hidden), BF16),
        ((n.micro * n.pairs, 2 * n.block, n.seq), F32),
        ((n.rows, n.width), F32),
        ((n.rows, n.width), F32),
        ((n.rows, 1), F32),
        ((n.rows, 1), F32),
    )


def dot(a, b):
    return jnp.dot(a, b, preferred_element_type=F32)


def dot_nt(a, b, precision=None):
    return lax.dot_general(a, b, (((1,), (1,)), ((), ())), precision=precision, preferred_element_type=F32)


def dot_tn(a, b, precision=None):
    return lax.dot_general(a, b, (((0,), (0,)), ((), ())), precision=precision, preferred_element_type=F32)


def iota(shape, dim):
    return lax.broadcasted_iota(jnp.int32, shape, dim)


def cols(at, size=TILE):
    return pl.ds(pl.multiple_of(at * size, size), size)


def bucket_of(offset):
    distance = jnp.abs(offset)
    bucket = jnp.minimum(distance, 8) + jnp.where(offset < 0, 16, 0)
    for bound_at in THRESHOLDS:
        bucket = bucket + jnp.where(distance >= bound_at, 1, 0)
    return bucket


def place_buckets(n):
    shape = (n.buckets, 2 * n.seq)
    at = iota(shape, 1)
    offset = jnp.where(at < n.seq, -at, 2 * n.seq - at)
    return jnp.where(bucket_of(offset) == iota(shape, 0), 1.0, 0.0)


def to_column(row, n):
    shape = (n.seq, n.seq)
    return jnp.sum(jnp.where(iota(shape, 0) == iota(shape, 1), row, 0.0), axis=1, keepdims=True)


def picked(order_col, n, place):
    return order_col[n.seq - n.query :] == place.astype(F32)


def bias_and_mask(n, v, bias):
    seq, query = n.seq, n.query
    base = dot_tn(v.rel_table[0], place_buckets(n), lax.Precision.HIGHEST)
    square = (seq, seq)
    row_at, col_at = iota(square, 0).astype(F32), iota(square, 1).astype(F32)
    visible_from = float(seq - query)
    content_sees, query_sees, chosen = [], [], []
    for b in range(n.micro):
        order_row = v.order[b : b + 1, :].astype(F32)
        order_col = to_column(order_row, n)
        rank_row = jnp.sum(jnp.where(order_col == col_at, row_at, 0.0), axis=0, keepdims=True)
        rank_col = to_column(rank_row, n)
        ends, total = [], jnp.int32(0)
        for d in range(v.lengths.shape[1]):
            total = total + v.lengths[b, d]
            ends.append(total)

        def doc_of(at):
            found = jnp.zeros(at.shape, F32)
            for end in ends:
                found = found + jnp.where(at >= end.astype(F32), 1.0, 0.0)
            return found

        doc_row = doc_of(iota((1, seq), 1).astype(F32))
        doc_col = doc_of(iota((seq, 1), 0).astype(F32))
        unmasked = rank_row < visible_from
        content_sees.append((doc_col == doc_row) & (unmasked | (rank_row <= rank_col)))
        at_place = picked(order_col, n, iota((query, seq), 1))
        place = order_col[seq - query :]
        rank = visible_from + iota((query, 1), 0).astype(F32)
        query_sees.append((doc_of(place) == doc_row) & (unmasked | (rank_row < rank) | at_place))
        chosen.append(jnp.where(at_place, 1.0, 0.0).astype(BF16))
    for h in range(n.heads):
        spread = jnp.broadcast_to(base[h : h + 1, :], (seq, 2 * seq))
        table = pltpu.roll(spread, 0, 1, stride=1, stride_axis=0)[:, :seq]
        high = table.astype(BF16)
        rest = table - high.astype(F32)
        middle = rest.astype(BF16)
        low = (rest - middle.astype(F32)).astype(BF16)
        for b in range(n.micro):
            of_query = dot(chosen[b], high) + dot(chosen[b], middle) + dot(chosen[b], low)
            start = (h % 2) * n.block
            bias[b * n.pairs + h // 2, start : start + seq, :] = jnp.where(content_sees[b], table, NEG_FILL)
            bias[b * n.pairs + h // 2, start + seq : start + n.block, :] = jnp.where(query_sees[b], of_query, NEG_FILL)


def half_masks():
    at = iota((1, LANES), 1)
    return jnp.where(at < LANES // 2, 1.0, 0.0).astype(BF16), jnp.where(at < LANES // 2, 0.0, 1.0).astype(BF16)


def both_heads(values):
    first, second = half_masks()
    return jnp.concatenate([values * first, values * second], axis=0)


def side_by_side(stacked):
    half = stacked.shape[0] // 2
    return jnp.concatenate([stacked[:half], stacked[half:]], axis=1)


def norm_rows(n, summed, spread_ref, gain, shift, write):
    step = n.block // 3

    @pl.loop(0, n.rows // step)
    def _(i):
        rows = pl.ds(pl.multiple_of(i * step, step), step)
        r = summed[rows, :]
        centered = r - jnp.mean(r, axis=1, keepdims=True)
        spread = lax.rsqrt(jnp.mean(centered * centered, axis=1, keepdims=True) + NORM_EPS)
        normed = centered * spread
        summed[rows, :] = normed
        spread_ref[rows, :] = spread
        write(rows, (normed * gain + shift).astype(BF16))


def norm_back(n, grad_of, normed_ref, spread_ref, gain, write):
    step = n.block // 3

    def body(i, sums):
        rows = pl.ds(pl.multiple_of(i * step, step), step)
        grad = grad_of(rows)
        normed = normed_ref[rows, :]
        scaled = grad * gain
        inner = jnp.mean(scaled * normed, axis=1, keepdims=True)
        back = spread_ref[rows, :] * (scaled - jnp.mean(scaled, axis=1, keepdims=True) - normed * inner)
        write(rows, back)
        low = back.astype(BF16).astype(F32)
        return (
            sums[0] + jnp.sum(grad * normed, axis=0, keepdims=True),
            sums[1] + jnp.sum(grad, axis=0, keepdims=True),
            sums[2] + jnp.sum(low, axis=0, keepdims=True),
        )

    zero = jnp.zeros((1, n.width), F32)
    return lax.fori_loop(0, n.rows // step, body, (zero, zero, zero))


def project(n, ready, w, v, s):
    width, tiles = n.width, n.width // TILE
    for i, matrix in enumerate((w.query, w.key, w.value)):
        ready(i)

        @pl.loop(0, tiles, unroll=True)
        def _(t):
            product = dot(s.left[:, :width], matrix[:, cols(t)])
            if i == 0:
                product = product + v.b_query[:, cols(t)]
            if i == 2:
                product = product + v.b_value[:, cols(t)]
            s.qkv[:, cols(i * tiles + t)] = product.astype(BF16)


def attend(n, s):
    factor = (LANES // 2) ** -0.5

    @pl.loop(0, n.micro * n.pairs, unroll=UNROLL)
    def _(it):
        b, pair = it // n.pairs, it % n.pairs
        rows = pl.ds(pl.multiple_of(b * n.block, 16), n.block)
        keys = pl.ds(pl.multiple_of(b * n.block, 16), n.seq)
        q = both_heads(s.qkv[rows, cols(pair, LANES)])
        k = s.qkv[keys, cols(n.pairs + pair, LANES)]
        val = both_heads(s.qkv[keys, cols(2 * n.pairs + pair, LANES)])
        scores = dot_nt(q, k) * factor + s.probs[it]
        powers = jnp.exp(scores - jnp.max(scores, axis=1, keepdims=True))
        probs = powers / jnp.sum(powers, axis=1, keepdims=True)
        s.probs[it] = probs
        mixed = dot(side_by_side(probs.astype(BF16)), val)
        s.left[rows, cols(n.pairs + pair, LANES)] = mixed.astype(BF16)


def attend_out(n, w, v, s):
    width, tiles = n.width, n.width // TILE

    @pl.loop(0, tiles, unroll=True)
    def _(t):
        product = dot(s.left[:, width : 2 * width], w.out[:, cols(t)])
        s.norm_attn[:, cols(t)] = s.left[:, cols(t)].astype(F32) + product + v.b_out[:, cols(t)]


def attend_norm(n, v, s):
    width = n.width

    def keep_h1(rows, value):
        s.left[rows, 2 * width : 3 * width] = value

    norm_rows(n, s.norm_attn, s.spread_attn, v.gain_attn[...], v.shift_attn[...], keep_h1)


def go_up(n, w, v, s):
    width, tiles, left_u = n.width, n.width // TILE, 3 * (n.width // TILE)
    step = n.block // 3
    c = (2 / math.pi) ** 0.5
    staged = s.norm_ffn

    def bend(t, i):
        for at in range(0, n.rows, step):
            rows = slice(at, at + step)
            z = staged[rows, i * TILE : (i + 1) * TILE] + v.b_up[:, cols(t)]
            square = z * z
            half = 0.5 + 0.5 * jnp.tanh(z * (c + 0.044715 * c * square))
            value = z * half
            s.left[rows, cols(left_u + t)] = value.astype(BF16)
            s.slope[rows, cols(t)] = (half + value * (1.0 - half) * (2.0 * c + 0.26829 * c * square)).astype(BF16)

    @pl.loop(0, n.hidden // width)
    def _(group):
        for i in range(tiles):
            staged[:, i * TILE : (i + 1) * TILE] = dot(s.left[:, 2 * width : 3 * width], w.up[:, cols(group * tiles + i)])
            if i:
                bend(group * tiles + i - 1, i - 1)
        bend(group * tiles + tiles - 1, tiles - 1)


def go_down(n, w, v, s):
    width, tiles = n.width, n.width // TILE

    @pl.loop(0, tiles, unroll=True)
    def _(t):
        product = dot(s.left[:, 3 * width :], w.down[:, cols(t)])
        s.norm_ffn[:, cols(t)] = s.left[:, cols(2 * tiles + t)].astype(F32) + product + v.b_down[:, cols(t)]


def ffn_norm(n, v, s, y):
    def keep_y(rows, value):
        y[rows, :] = value

    norm_rows(n, s.norm_ffn, s.spread_ffn, v.gain_ffn[...], v.shift_ffn[...], keep_y)


def ffn_norm_back(n, v, s, dy, right, smalls, resid):
    width = n.width
    df_cols = slice(4 * width + n.hidden, 5 * width + n.hidden)

    def keep_df(rows, value):
        resid[rows, :] = value
        right[rows, df_cols] = value.astype(BF16)

    gain, shift, low = norm_back(n, lambda rows: dy[rows, :].astype(F32), s.norm_ffn, s.spread_ffn, v.gain_ffn[...], keep_df)
    smalls[10:11, :], smalls[11:12, :], smalls[9:10, :] = gain, shift, low


def down_back(n, w, s, right, smalls, sent):
    width, tiles = n.width, n.width // TILE
    df_cols = slice(4 * width + n.hidden, 5 * width + n.hidden)
    step = n.block // 3
    staged = s.norm_ffn

    def bend(group, i):
        t = group * tiles + i
        total = jnp.zeros((8, TILE), F32)
        for at in range(0, n.rows, step):
            rows = slice(at, at + step)
            dz = (staged[rows, i * TILE : (i + 1) * TILE] * s.slope[rows, cols(t)].astype(F32)).astype(BF16)
            right[rows, cols(4 * tiles + t)] = dz
            total = total + jnp.sum(dz.astype(F32).reshape(step // 8, 8, TILE), axis=0)
        smalls[pl.ds(5 + group, 1), cols(i)] = jnp.sum(total, axis=0, keepdims=True)

    @pl.loop(0, n.hidden // width)
    def _(group):
        for i in range(tiles):
            staged[:, i * TILE : (i + 1) * TILE] = dot_nt(right[:, df_cols], w.down[cols(group * tiles + i), :])
            if i:
                bend(group, i - 1)
        bend(group, tiles - 1)
        sent(group)


def up_back(n, w, dy, right, resid):
    width, tiles = n.width, n.width // TILE

    @pl.loop(0, tiles, unroll=True)
    def _(t):
        spread = dot_nt(right[:, 4 * width : 4 * width + n.hidden], w.up[cols(t), :])
        dy[:, cols(t)] = (spread + resid[:, cols(t)]).astype(BF16)


def attend_norm_back(n, v, s, dy, right, smalls, resid):
    width = n.width

    def keep_da(rows, value):
        resid[rows, :] = value
        right[rows, 3 * width : 4 * width] = value.astype(BF16)

    gain, shift, low = norm_back(n, lambda rows: dy[rows, :].astype(F32), s.norm_attn, s.spread_attn, v.gain_attn[...], keep_da)
    smalls[3:4, :], smalls[4:5, :], smalls[2:3, :] = gain, shift, low


def out_back(n, w, dy, right):
    width, tiles = n.width, n.width // TILE

    @pl.loop(0, tiles, unroll=True)
    def _(t):
        dy[:, cols(t)] = dot_nt(right[:, 3 * width : 4 * width], w.out[cols(t), :]).astype(BF16)


def attend_back(n, v, s, dy, right, smalls, table_sum, chosen, between):
    width = n.width
    factor = (LANES // 2) ** -0.5
    table_sum[...] = jnp.zeros(table_sum.shape, F32)
    square = (n.seq, n.seq)
    same = jnp.where(iota(square, 0) + iota(square, 1) == n.seq - 1, 1.0, 0.0).astype(BF16)
    for b in range(n.micro):
        order_col = to_column(v.order[b : b + 1, :].astype(F32), n)
        predicted = picked(order_col, n, n.seq - 1 - iota((n.query, n.seq), 1))
        chosen[b, : n.seq, :] = same
        chosen[b, n.seq :, :] = jnp.where(predicted, 1.0, 0.0).astype(BF16)

    @pl.loop(0, n.micro * n.pairs // UNROLL)
    def _(outside):
        for inside in range(UNROLL):
            it = outside * UNROLL + inside
            b, pair = it // n.pairs, it % n.pairs
            start = b * n.block
            rows = pl.ds(pl.multiple_of(start, 16), n.block)
            keys = pl.ds(pl.multiple_of(start, 16), n.seq)
            rest = pl.ds(pl.multiple_of(start + n.seq, 16), n.query)
            grad = both_heads(dy[rows, cols(pair, LANES)])
            q = both_heads(s.qkv[rows, cols(pair, LANES)])
            k = both_heads(s.qkv[keys, cols(n.pairs + pair, LANES)])
            val = s.qkv[keys, cols(2 * n.pairs + pair, LANES)]
            probs = s.probs[it]
            grad_probs = dot_nt(grad, val)
            inner = jnp.sum(probs * grad_probs, axis=1, keepdims=True)
            grad_scores = (probs * (grad_probs - inner)).astype(BF16)
            right[rows, cols(pair, LANES)] = (dot(side_by_side(grad_scores), k) * factor).astype(BF16)
            right[keys, cols(n.pairs + pair, LANES)] = (dot_tn(grad_scores, q) * factor).astype(BF16)
            right[keys, cols(2 * n.pairs + pair, LANES)] = dot_tn(probs.astype(BF16), grad).astype(BF16)
            none = jnp.zeros((n.query, LANES), BF16)
            right[rest, cols(n.pairs + pair, LANES)] = none
            right[rest, cols(2 * n.pairs + pair, LANES)] = none
            for half in range(2):
                of_head = grad_scores[half * n.block : (half + 1) * n.block]
                table_sum[2 * pair + half] += dot_tn(chosen[b], of_head)
        between(outside)

    smalls[0:1, :] = jnp.sum(right[:, :width].astype(F32), axis=0, keepdims=True)
    smalls[1:2, :] = jnp.sum(right[:, 2 * width : 3 * width].astype(F32), axis=0, keepdims=True)


def table_back(n, smalls, table_sum):
    by_place = []
    for h in range(n.heads):
        wide = jnp.concatenate([table_sum[h], jnp.zeros((n.seq, n.seq), F32)], axis=1)
        turned = pltpu.roll(wide, n.seq + 1, 1, stride=1, stride_axis=0)
        by_place.append(jnp.sum(turned, axis=0, keepdims=True))
    by_place = jnp.concatenate(by_place, axis=0)
    smalls[12 : 12 + n.heads, : n.buckets] = dot_nt(by_place, place_buckets(n), lax.Precision.HIGHEST)


def inputs_back(n, w, right, resid, dx):
    width, tiles = n.width, n.width // TILE

    @pl.loop(0, tiles, unroll=True)
    def _(t):
        total = resid[:, cols(t)]
        for i, matrix in enumerate((w.query, w.key, w.value)):
            total = total + dot_nt(right[:, i * width : (i + 1) * width], matrix[cols(t), :])
        dx[:, cols(t)] = total.astype(BF16)


def tiles_of(n, core):
    tiles, groups = n.width // TILE, n.hidden // n.width
    down = groups * tiles // 2

    def ffn(i):
        is_down = i < down
        up = i - down
        left = jnp.where(is_down, 3 * tiles + core * down + i, 2 * tiles + up % tiles)
        return left, jnp.where(is_down, 4 + groups, 4 + core * (groups // 2) + up // tiles)

    def attention(i):
        group = i // tiles
        return i % tiles + jnp.where(core * group == 1, tiles, 0), 2 * core + group

    return (ffn, 2 * down), (attention, 2 * tiles)


def weight_grads(n, of, count, first, left, right, packed):
    per = TILE // packed.shape[2] // packed.shape[1]
    by = math.gcd(count, UNROLL)

    @pl.loop(0, count // by)
    def _(outside):
        for inside in range(by):
            i = outside * by + inside
            left_tile, group = of(i)
            rhs = right[:, pl.ds(pl.multiple_of(group * n.width, n.width), n.width)]
            product = dot_tn(left[:, cols(left_tile)], rhs).astype(BF16)
            packed[pl.ds((first + i) * per, per)] = product.reshape((per,) + packed.shape[1:])


class Landing(NamedTuple):
    from_y: Any
    end_b: Any
    end_a: Any
    mid_a: Any
    mid_b: Any
    rung_b: Any


class Arrival(NamedTuple):
    y: Any
    end_b: Any
    end_a: Any
    mid_a: Any
    mid_b: Any
    rung: Any
    own_a: Any
    own_b: Any
    end_final: Any
    y_final: Any
    mid_final: Any
    end_both: Any
    sibling: Any


class Place(NamedTuple):
    core: Any
    y: Any
    mine: Any
    other: Any
    is_end: Any
    is_mid: Any
    sibling: Any
    y_peer: Any
    z_in: Any
    z_out: Any
    z_mid: Any
    across: Any
    doubling: Any


def find_place():
    pipe, index = lax.axis_index("pipe"), lax.axis_index("dp")
    base, local = index // 16 * 16, index % 16
    z, y, core = local // 4, local // 2 % 2, local % 2

    def at(zz, yy, cc):
        return (pipe, base + zz * 4 + yy * 2 + cc)

    return Place(
        core,
        y,
        z + 1,
        4 - z,
        (z == 0) | (z == 3),
        (z == 1) | (z == 2),
        at(z, y, 1 - core),
        at(z, 1 - y, core),
        at(jnp.where(z == 0, 1, 2), y, core),
        at(jnp.where(z == 1, 0, 3), y, core),
        at(3 - z, y, core),
        (1 - pipe, index),
        [(pipe, base + jnp.bitwise_xor(local, 1 << j)) for j in range(4)],
    )


def greet_all(me):
    barrier = pltpu.get_barrier_semaphore()
    for device in me.doubling + [me.across]:
        pl.semaphore_signal(barrier, inc=1, device_id=device, device_id_type=MESH)

    @pl.when(me.is_mid)
    def _():
        pl.semaphore_signal(barrier, inc=1, device_id=me.z_mid, device_id_type=MESH)
        pl.semaphore_wait(barrier, 6)

    @pl.when(me.is_end)
    def _():
        pl.semaphore_wait(barrier, 5)


def remote(src, dst, send, recv, device):
    return pltpu.make_async_remote_copy(src_ref=src, dst_ref=dst, send_sem=send, recv_sem=recv, device_id=device, device_id_type=MESH)


def wait_for(ref, sem):
    pltpu.make_async_copy(ref, ref, sem).wait()


def added(a, b):
    return (a.astype(F32) + b.astype(F32)).astype(BF16)


def sums(me, packed, out, land, sem, send):
    steps = packed.shape[0]
    c, y, mine, other = me.core, me.y, me.mine, me.other
    both = pl.ds(2, 2)

    def s0(k):
        remote(packed.at[k, 1 - y], land.from_y.at[k], send.at[0], sem.y.at[k], me.y_peer).start()

        @pl.when(me.is_end)
        def _():
            remote(packed.at[k, both], land.end_b.at[k], send.at[1], sem.end_b.at[k], me.z_in).start()

    def s1(k):
        wait_for(land.from_y.at[k], sem.y.at[k])
        packed[k, y] = added(packed[k, y], land.from_y[k])

        @pl.when(me.is_end)
        def _():
            remote(packed.at[k, y], land.end_a.at[k], send.at[2], sem.end_a.at[k], me.z_in).start()

        @pl.when(me.is_mid)
        def _():
            wait_for(land.end_b.at[k], sem.end_b.at[k])
            packed[k, both] = added(packed[k, both], land.end_b[k])
            remote(packed.at[k, other], land.mid_b.at[k], send.at[3], sem.mid_b.at[k], me.z_mid).start()

    def s2(k):
        @pl.when(me.is_mid)
        def _():
            wait_for(land.end_a.at[k], sem.end_a.at[k])
            packed[k, y] = added(packed[k, y], land.end_a[k])
            remote(packed.at[k, y], land.mid_a.at[k], send.at[4], sem.mid_a.at[k], me.z_mid).start()
            wait_for(land.mid_b.at[k], sem.mid_b.at[k])
            packed[k, mine] = added(packed[k, mine], land.mid_b[k])
            remote(packed.at[k, mine], land.rung_b.at[k], send.at[5], sem.rung.at[k], me.y_peer).start()

    def s3(k):
        @pl.when(me.is_mid)
        def _():
            wait_for(land.mid_a.at[k], sem.mid_a.at[k])
            total = land.from_y.at[k]
            total[...] = added(packed[k, y], land.mid_a[k])
            remote(total, out.at[c, k, y], send.at[6], sem.end_final.at[k], me.z_out).start()
            remote(total, out.at[c, k, y], send.at[7], sem.y_final.at[k], me.y_peer).start()
            pltpu.make_async_copy(total, out.at[c, k, y], sem.own_a.at[k]).start()
            wait_for(land.rung_b.at[k], sem.rung.at[k])
            total = land.end_a.at[k]
            total[...] = added(packed[k, mine], land.rung_b[k])
            remote(total, out.at[c, k, mine], send.at[8], sem.mid_final.at[k], me.z_mid).start()
            pltpu.make_async_copy(total, out.at[c, k, mine], sem.own_b.at[k]).start()

    def s4(k):
        @pl.when(me.is_end)
        def _():
            wait_for(out.at[c, k, y], sem.end_final.at[k])
            remote(out.at[c, k, y], out.at[c, k, y], send.at[7], sem.y_final.at[k], me.y_peer).start()

        @pl.when(me.is_mid)
        def _():
            wait_for(out.at[c, k, other], sem.mid_final.at[k])
            wait_for(out.at[c, k, mine], sem.own_b.at[k])
            remote(out.at[c, k, both], out.at[c, k, both], send.at[9], sem.end_both.at[k], me.z_out).start()

    def s5(k):
        wait_for(out.at[c, k, 1 - y], sem.y_final.at[k])

        @pl.when(me.is_end)
        def _():
            wait_for(out.at[c, k, both], sem.end_both.at[k])

        @pl.when(me.is_mid)
        def _():
            wait_for(out.at[c, k, y], sem.own_a.at[k])

        remote(out.at[c, k], out.at[c, k], send.at[10], sem.sibling.at[k], me.sibling).start()

    def s6(k):
        wait_for(out.at[1 - c, k], sem.sibling.at[k])

    stages = (s0, s1, s2, s3, s4, s5, s6)

    def slot(t):
        for i, stage in enumerate(stages):
            k = t - i * LAG

            @pl.when((k >= 0) & (k < steps))
            def _():
                stage(jnp.clip(k, 0, steps - 1))

    def finish():
        section = land.from_y
        wait_for(section, send.at[0])
        wait_for(section, send.at[7])
        wait_for(packed, send.at[10])

        @pl.when(me.is_end)
        def _():
            wait_for(land.end_b, send.at[1])
            wait_for(section, send.at[2])

        @pl.when(me.is_mid)
        def _():
            for which in (3, 4, 5, 6, 8):
                wait_for(section, send.at[which])
            wait_for(land.end_b, send.at[9])

    return slot, steps + (len(stages) - 1) * LAG, finish


def small_sums(me, smalls, held, total, recv, send):
    def source(j):
        return smalls if j == 0 else held.at[1, j - 1]

    def copy(j):
        return remote(source(j), held.at[0, j], send.at[j], recv.at[j], me.doubling[j])

    def step(j):
        if j >= 0:
            copy(j).wait()
            summed = source(j)[...] + held[0, j]
            if j == 3:
                total[...] = summed
            else:
                held[1, j] = summed
        if j < 3:
            copy(j + 1).start()

    return step


def copies_of(pairs, sems):
    return [pltpu.make_async_copy(src, dst, sems.at[i]) for i, (src, dst) in enumerate(pairs)]


def bucket_rows(n, content, query, wide):
    pairs = []
    for b in range(n.micro):
        pairs.append((content.at[0, pl.ds(b * n.seq, n.seq)], wide.at[pl.ds(b * n.block, n.seq)]))
        pairs.append((query.at[0, pl.ds(b * n.query, n.query)], wide.at[pl.ds(b * n.block + n.seq, n.query)]))
    return pairs


def whole_kernel(n, *refs):
    content, query, *refs = refs
    w_hbm, refs = Weights(*refs[:6]), refs[6:]
    v, refs = Vectors(*refs[:12]), refs[12:]
    content_out, query_out, out, total, *refs = refs
    w, refs = Weights(*refs[:6]), refs[6:]
    left, right, y, dx, dy, resid, table_sum, chosen, smalls, held, packed, *refs = refs
    s, refs = State(left.at[pl.ds(0, n.rows)], *refs[:7]), refs[7:]
    land, refs = Landing(*refs[:6]), refs[6:]
    arrive, refs = Arrival(*refs[:13]), refs[13:]
    w_sem, in_sem, grad_sem, out_sem, pipe_send, pipe_recv, core_send, core_recv, small_send, small_recv, sum_send = refs
    width, rows = n.width, n.rows
    inputs = s.left.at[:, pl.ds(0, width)]
    mine_right = right.at[pl.ds(0, rows)]
    groups = n.hidden // width
    first, last = lax.axis_index("pipe") == 0, lax.axis_index("pipe") == 1
    me = find_place()

    weights = copies_of([(a.at[0], b) for a, b in zip(w_hbm, w)], w_sem)
    own_rows = copies_of(bucket_rows(n, content, query, inputs), in_sem)
    own_grads = copies_of(bucket_rows(n, content, query, dy), in_sem)

    @pl.when(first)
    def _():
        for cp in own_rows:
            cp.start()

    @pl.when(last)
    def _():
        for cp in own_grads:
            cp.start()

    for cp in weights:
        cp.start()
    greet_all(me)
    bias_and_mask(n, v, s.probs)
    hand_up = remote(y, inputs, pipe_send, pipe_recv, me.across)
    hand_down = remote(dx, dy, pipe_send, pipe_recv, me.across)

    def to_core(which, src, dst):
        return remote(src, dst, core_send.at[which], core_recv.at[which], me.sibling)

    def left_copy(which, at, size):
        return to_core(which, left.at[pl.ds(0, rows), pl.ds(at, size)], left.at[pl.ds(rows, rows), pl.ds(at, size)])

    def right_copy(which, at, size):
        return to_core(which, right.at[pl.ds(0, rows), pl.ds(at, size)], right.at[pl.ds(rows, rows), pl.ds(at, size)])

    share_left = left_copy(0, 0, 3 * width + n.hidden)
    share_attention = right_copy(1, 0, 3 * width)
    share_da = right_copy(2, 3 * width, width)
    share_df = right_copy(3, (4 + groups) * width, width)

    def share_dz(group):
        return right_copy(4 + group, pl.multiple_of((4 + group) * width, width), width)

    @pl.when(first)
    def _():
        for cp in own_rows:
            cp.wait()

    @pl.when(last)
    def _():
        hand_up.wait_recv()

    done = set()

    def ready(i):
        if i not in done:
            done.add(i)
            weights[i].wait()

    project(n, ready, w, v, s)
    attend(n, s)
    ready(3)
    attend_out(n, w, v, s)
    attend_norm(n, v, s)
    ready(4)
    go_up(n, w, v, s)
    ready(5)
    go_down(n, w, v, s)
    ffn_norm(n, v, s, y)

    @pl.when(first)
    def _():
        hand_up.start()

    share_left.start()
    results = copies_of([(b, a) for a, b in bucket_rows(n, content_out, query_out, y)], out_sem)
    results_back = copies_of([(b, a) for a, b in bucket_rows(n, content_out, query_out, dx)], out_sem)

    @pl.when(last)
    def _():
        for cp in results:
            cp.start()
        for cp in own_grads:
            cp.wait()

    @pl.when(first)
    def _():
        hand_up.wait_send()
        hand_down.wait_recv()

    slot, slots, finish = sums(me, packed, out, land, arrive, sum_send)
    (ffn, ffn_count), (attention, attention_count) = tiles_of(n, me.core)
    ffn_norm_back(n, v, s, dy, mine_right, smalls, resid)
    share_df.start()
    down_back(n, w, s, mine_right, smalls, lambda group: share_dz(group).start())
    up_back(n, w, dy, mine_right, resid)

    def ffn_grads():
        share_left.wait_recv()
        share_df.wait_recv()
        for group in range(groups):
            share_dz(group).wait_recv()
        weight_grads(n, ffn, ffn_count, 0, left, right, packed)

    pl.when(first)(ffn_grads)
    attend_norm_back(n, v, s, dy, mine_right, smalls, resid)
    share_da.start()
    out_back(n, w, dy, mine_right)
    early = n.micro * n.pairs // UNROLL * EARLY

    def between(outside):
        @pl.when(first)
        def _():
            @pl.loop(0, EARLY)
            def _(i):
                slot(outside * EARLY + i)

    attend_back(n, v, s, dy, mine_right, smalls, table_sum, chosen, between)
    share_attention.start()
    inputs_back(n, w, mine_right, resid, dx)

    @pl.when(last)
    def _():
        hand_down.start()

    table_back(n, smalls, table_sum)
    small_step = small_sums(me, smalls, held, total, small_recv, small_send)
    small_step(-1)

    @pl.when(first)
    def _():
        for cp in results_back:
            cp.start()

    pl.when(last)(ffn_grads)
    share_attention.wait_recv()
    share_da.wait_recv()
    weight_grads(n, attention, attention_count, ffn_count, left, right, packed)
    start = jnp.where(first, early, 0)

    @pl.loop(0, slots - start)
    def _(i):
        slot(start + i)
        for j in range(4):
            pl.when(i == 4 * (j + 1))(functools.partial(small_step, j))

    finish()
    for which in [share_left, share_attention, share_da, share_df] + [share_dz(group) for group in range(groups)]:
        which.wait_send()
    for cp in results:
        cp.wait()

    @pl.when(last)
    def _():
        hand_down.wait_send()


def shaped(shape, dtype=BF16):
    return jax.ShapeDtypeStruct(shape, dtype)


def run_layers(n, content, query, w, v):
    rows, width = n.rows, n.width
    vmem, smem, anywhere = (pl.BlockSpec(memory_space=space) for space in (pltpu.VMEM, pltpu.SMEM, pl.ANY))
    dma = pltpu.SemaphoreType.DMA
    steps = (4 * width + 2 * n.hidden) // (2 * 4 * CHUNK)
    half = (steps, 4, CHUNK, width)
    section, sections = pltpu.VMEM((steps, CHUNK, width), BF16), pltpu.VMEM((steps, 2, CHUNK, width), BF16)
    small_shape = (24, width)
    left, *others = state_shapes(n)
    scratch = [pltpu.VMEM(m.shape[1:], BF16) for m in w]
    scratch += [
        pltpu.VMEM((2 * rows, left[0][1]), BF16),
        pltpu.VMEM((2 * rows, 5 * width + n.hidden), BF16),
        pltpu.VMEM((rows, width), BF16),
        pltpu.VMEM((rows, width), BF16),
        pltpu.VMEM((rows, width), BF16),
        pltpu.VMEM((rows, width), F32),
        pltpu.VMEM((n.heads, n.seq, n.seq), F32),
        pltpu.VMEM((n.micro, n.block, n.seq), BF16),
        pltpu.VMEM(small_shape, F32),
        pltpu.VMEM((2, 4) + small_shape, F32),
        pltpu.VMEM(half, BF16),
    ]
    scratch += [pltpu.VMEM(shape, dtype) for shape, dtype in others]
    scratch += [section, sections, section, section, section, section]
    scratch += [dma((steps,))] * 13
    shares = 4 + n.hidden // width
    scratch += [dma((6,)), dma((2 * n.micro,)), dma((2 * n.micro,)), dma((2 * n.micro,)), dma, dma, dma((shares,)), dma((shares,)), dma((4,)), dma((4,)), dma((11,))]
    return pl.pallas_call(
        functools.partial(whole_kernel, n),
        out_shape=[shaped(content.shape), shaped(query.shape), shaped((2,) + half), shaped(small_shape, F32)],
        in_specs=[anywhere] * 8 + [vmem] * 10 + [smem, vmem],
        out_specs=[anywhere] * 3 + [vmem],
        scratch_shapes=scratch,
        compiler_params=pltpu.CompilerParams(collective_id=1, has_side_effects=True, vmem_limit_bytes=VMEM_LIMIT),
    )(content, query, *w, *v)


def unpack(n, packed, smalls):
    width, heads = n.width, n.heads
    groups = n.hidden // width
    half_down, half_groups = n.hidden // 2, groups // 2
    halves = [packed[core].reshape(-1, width) for core in range(2)]
    down = jnp.concatenate([half[:half_down] for half in halves], axis=0).astype(F32)[None]
    blocks = [[half[half_down + i * width : half_down + (i + 1) * width] for i in range(half_groups + 2)] for half in halves]
    up = jnp.concatenate(blocks[0][:half_groups] + blocks[1][:half_groups], axis=1).astype(F32)[None]
    query, key, value, out = (block.astype(F32)[None] for block in blocks[0][half_groups:] + blocks[1][half_groups:])
    vectors = [smalls[i : i + 1] for i in range(5)]
    vectors.append(smalls[5 : 5 + groups].reshape(1, n.hidden))
    vectors += [smalls[i : i + 1] for i in (9, 10, 11)]
    vectors.append(smalls[12 : 12 + heads, : n.buckets].T[None])
    return (query, key, value, out, up, down), vectors


def across_blocks(packed, smalls):
    blocks = lax.axis_size("dp") // 16
    if blocks > 1:
        groups = [[block * 16 + i for block in range(blocks)] for i in range(16)]
        packed = lax.psum(packed.astype(F32), "dp", axis_index_groups=groups)
        smalls = lax.psum(smalls, "dp", axis_index_groups=groups)
    return packed, smalls


def on_device(content_ends, query_ends, w_query, b_query, w_key, w_value, b_value, w_out, b_out, gain_attn, shift_attn, w_up, b_up, w_down, b_down, gain_ffn, shift_ffn, rel_table, doc_lengths, position_order):
    micro, seq = position_order.shape
    n = Sizes(micro, seq, query_ends.shape[1] // micro, content_ends.shape[2], rel_table.shape[2], w_up.shape[2], rel_table.shape[1])
    w = Weights(w_query, w_key, w_value, w_out, w_up, w_down)
    v = Vectors(b_query, b_value, b_out, gain_attn, shift_attn, b_up, b_down, gain_ffn, shift_ffn, rel_table, doc_lengths, position_order)
    content_out, query_out, packed, smalls = run_layers(n, content_ends, query_ends, w, v)
    packed, smalls = across_blocks(packed, smalls)
    g, d = unpack(n, packed, smalls)
    return content_out, query_out, g[0], d[0], g[1], g[2], d[1], g[3], d[2], d[3], d[4], g[4], d[5], g[5], d[6], d[7], d[8], d[9]


def solution(mesh):
    rows, matrix, vector, buckets = P("pipe", "dp", None), P("pipe", None, None), P("pipe", None), P("dp", None)
    grads = (matrix, vector, matrix, matrix, vector, matrix, vector, vector, vector, matrix, vector, matrix, vector, vector, vector, matrix)
    return jax.shard_map(on_device, mesh=mesh, in_specs=(rows, rows, *grads, buckets, buckets), out_specs=(rows, rows, *grads), check_vma=False)
```

time: 318 us -> 260 us (0.82)
  waiting for transfers between devices: 66 us -> 0 us
  Pallas kernels: 222 us -> 231 us
  local copies, waits for them, and re-layouts: 9 us -> 13.8 us
    ppermute x2 -> x0, waiting for transfers between devices: 66 us -> none  [the longest x1 55.5 us: run_layers(): returned = lax.ppermute(dx1, 'pipe', [(1, 0)])]
    convert_element_type x1 -> x4, other arithmetic: 4.32 us -> 14.2 us  [the longest x2 5.39 us: unpack(): block.astype(F32)[None]]
    pallas_call x4 -> x1, Pallas kernels: 222 us -> 231 us  [run_layers(): pl.pallas_call(functools.partial(whole_kernel, n), out_shape=[shaped(cont...]
    broadcast_in_dim x1 -> x0, other arithmetic: 8.01 us -> none  [unpack(): whole.append(packed[(4 + groups) * width:].astype(F32)[None])]
    slice x1 -> x3, local copies, waits for them, and re-layouts: 1.54 us -> 8.35 us  [the longest x1 4.11 us: unpack(): half[half_down + i * width:half_down + (i + 1) * width]]
    slice x1 -> x0, other arithmetic: 3.77 us -> none  [unpack(): parts[4 + i]]
  transfers between devices with their start and end apart: 2 -> 0, of which waited for: 2 -> 0; matrix products, arithmetic and copies ran while one was open for 0% -> 0% of each run, Pallas kernels for 0% -> 0%
where the time goes in v1:
time: 260 us
  Pallas kernels  231 us (89%)
  other arithmetic  14.2 us (5%)
  local copies, waits for them, and re-layouts  13.8 us (5%)
    pallas_call x1, Pallas kernels, run_layers(): pl.pallas_call(functools.partial(whole_kernel, n), out_shape=[shaped(cont...  231 us
    convert_element_type x2, other arithmetic, unpack(): block.astype(F32)[None]  5.39 us

profile of v1, /device:TPU:0, one launch (start us, length us, event | category | flops | bytes accessed | tf_op | source)
XLA Modules:
  0.0 260.1 jit_solution(13106586144822462744)
XLA Ops:
  0.7 1.4 copy.38.refs_17_
  2.0 231.4 %shard_map.331 = (bf16[1,256,768]{2,1,0:T(8,128)(2,1)}, bf16[1,32,768]{2,1,0:T(8,128)(2,1)}, bf16[2,72,4,16,768]{4,3,2,1,0:T(8,128)(2,1)}, f32[24,768]{1,0:T(8,128)}) custom-call(bf16[1,256,768]{2,1,0:T(8,128)(2,1)} %refs_0_.1, bf16[1,32,768]{2,1,0:T(8,128)(2,1)} %refs_1_.1, bf16[1,768,768]{2,1,0:T(8,128)(2,1)} %refs_2_.1, bf16[1,768,768]{2,1,0:T(8,128)(2,1)} %refs_3_.1, ...), custom_call_target="tpu_custom_call" | custom-call | tf_op jit(solution)/shard_map/pallas_call | solution.py:931
  233.5 0.7 slice_bitcast_fusion.1
  234.2 0.6 copy.39
  234.8 0.8 slice_bitcast_fusion
  235.6 1.6 fusion.2
  237.1 0.6 copy.40
  237.7 2.7 %fusion = (bf16[1,24,4,16,768]{4,3,2,1,0:T(8,128)(2,1)S(1)}, bf16[1,24,4,16,768]{4,3,2,1,0:T(8,128)(2,1)S(1)}) fusion(bf16[2,72,4,16,768]{4,3,2,1,0:T(8,128)(2,1)} %get-tuple-element.24), kind=kLoop, calls=%fused_computation.8 | loop fusion | bytes 9437184 | tf_op jit(solution)/shard_map/slice | solution.py:946
  240.4 4.1 %fusion.1 = (bf16[1,12,4,16,768]{4,3,2,1,0:T(8,128)(2,1)S(1)}, bf16[1,12,4,16,768]{4,3,2,1,0:T(8,128)(2,1)S(1)}, bf16[1,12,4,16,768]{4,3,2,1,0:T(8,128)(2,1)S(1)...) fusion(bf16[2,72,4,16,768]{4,3,2,1,0:T(8,128)(2,1)} %get-tuple-, ...), kind=kLoop, calls=%fused_computation.9 | loop fusion | bytes 18874368 | tf_op jit(solution)/shard_map/slice | solution.py:947
  244.5 4.5 %maximum_convert_fusion.1 = f32[1,3072,768]{2,1,0:T(8,128)} fusion(bf16[1,1536,768]{2,1,0:T(8,128)(2,1)S(1)} %bitcast.27, bf16[1,1536,768]{2,1,0:T(8,128)(2,1)S(1)} %bitcast.26), kind=kLoop, calls=%fused_computation.1 | loop fusion | flops 9437184 | bytes 14155776 | tf_op jit(solution)/shard_map/convert_element_type | solution.py:946
  249.0 4.3 %maximum_convert_fusion = f32[1,768,3072]{2,1,0:T(8,128)} fusion(bf16[1,768,768]{2,1,0:T(8,128)(2,1)S(1)} %bitcast.29, bf16[1,768,768]{2,1,0:T(8,128)(2,1)S(1)} %bitcast.30, bf16[1,768,768]{2,1,0:T(8,128)(2,1)S(1)} %bitcast.31, bf16[1,768,768]{2,1,0:T(8,128)(2,1)S(1)} %bitcast.28), kind=kLoop, calls=%fused_computation | loop fusion | flops 18874368 | bytes 14155776 | tf_op jit(solution)/shard_map/convert_element_type | solution.py:948
  253.3 2.7 %bitcast_convert_fusion = (f32[1,768,768]{2,1,0:T(8,128)}, f32[1,768,768]{2,1,0:T(8,128)}) fusion(bf16[1,12,4,16,768]{4,3,2,1,0:T(8,128)(2,1)S(1)} %get-tuple-element.50, bf16[1,12,4,16,768]{4,3,2,1,0:T(8,128)(2,1)S(1)} %get-tuple-element.51), kind=kLoop, calls=%fused_computation.2 | loop fusion | flops 1179648 | bytes 7077888 | tf_op jit(solution)/shard_map/convert_element_type | solution.py:949
  256.0 0.0 copy-start
  256.0 0.0 copy-start.1
  256.0 2.7 %bitcast_convert_fusion.2 = (f32[1,768,768]{2,1,0:T(8,128)}, f32[1,768,768]{2,1,0:T(8,128)}) fusion(bf16[1,12,4,16,768]{4,3,2,1,0:T(8,128)(2,1)S(1)} %get-tuple-element.52, bf16[1,12,4,16,768]{4,3,2,1,0:T(8,128)(2,1)S(1)} %get-tuple-element.53), kind=kLoop, calls=%fused_computation.4 | loop fusion | flops 1179648 | bytes 7077888 | tf_op jit(solution)/shard_map/convert_element_type | solution.py:949
  258.7 0.0 copy-done
  258.7 0.7 copy.43
  259.5 0.0 copy-done.1
  259.5 0.6 copy.44
Async XLA Ops:
  256.0 2.7 %copy-start = (bf16[1,256,768]{2,1,0:T(8,128)(2,1)S(1)}, bf16[1,256,768]{2,1,0:T(8,128)(2,1)}, u32[]{:S(2)}) copy-start(bf16[1,256,768]{2,1,0:T(8,128)(2,1)} %get-tuple-element.84) | copy-start | bytes 1179652
  256.0 3.4 %copy-start.1 = (bf16[1,32,768]{2,1,0:T(8,128)(2,1)S(1)}, bf16[1,32,768]{2,1,0:T(8,128)(2,1)}, u32[]{:S(2)}) copy-start(bf16[1,32,768]{2,1,0:T(8,128)(2,1)} %get-tuple-element.85) | copy-start | bytes 147460

commit v2 on v1

--- a/solution.py
+++ b/solution.py
@@ -20,6 +20,7 @@
 UNROLL = 3
 EARLY = 3
 LAG = 2
+RING = 16
 CHUNK = 16
 VMEM_LIMIT = 63 * 2**20
 
@@ -102,8 +103,8 @@
     return lax.dot_general(a, b, (((1,), (1,)), ((), ())), precision=precision, preferred_element_type=F32)
 
 
-def dot_tn(a, b, precision=None):
-    return lax.dot_general(a, b, (((0,), (0,)), ((), ())), precision=precision, preferred_element_type=F32)
+def dot_tn(a, b):
+    return lax.dot_general(a, b, (((0,), (0,)), ((), ())), preferred_element_type=F32)
 
 
 def iota(shape, dim):
@@ -140,7 +141,8 @@
 
 def bias_and_mask(n, v, bias):
     seq, query = n.seq, n.query
-    base = dot_tn(v.rel_table[0], place_buckets(n), lax.Precision.HIGHEST)
+    by_head = jnp.concatenate([v.rel_table[h] for h in range(n.heads)], axis=0)
+    base = jnp.dot(by_head, place_buckets(n), precision=lax.Precision.HIGHEST, preferred_element_type=F32)
     square = (seq, seq)
     row_at, col_at = iota(square, 0).astype(F32), iota(square, 1).astype(F32)
     visible_from = float(seq - query)
@@ -590,78 +592,78 @@
     both = pl.ds(2, 2)
 
     def s0(k):
-        remote(packed.at[k, 1 - y], land.from_y.at[k], send.at[0], sem.y.at[k], me.y_peer).start()
+        remote(packed.at[k, 1 - y], land.from_y.at[k], send.at[0], sem.y.at[jnp.bitwise_and(k, RING - 1)], me.y_peer).start()
 
         @pl.when(me.is_end)
         def _():
-            remote(packed.at[k, both], land.end_b.at[k], send.at[1], sem.end_b.at[k], me.z_in).start()
+            remote(packed.at[k, both], land.end_b.at[k], send.at[1], sem.end_b.at[jnp.bitwise_and(k, RING - 1)], me.z_in).start()
 
     def s1(k):
-        wait_for(land.from_y.at[k], sem.y.at[k])
+        wait_for(land.from_y.at[k], sem.y.at[jnp.bitwise_and(k, RING - 1)])
         packed[k, y] = added(packed[k, y], land.from_y[k])
 
         @pl.when(me.is_end)
         def _():
-            remote(packed.at[k, y], land.end_a.at[k], send.at[2], sem.end_a.at[k], me.z_in).start()
+            remote(packed.at[k, y], land.end_a.at[k], send.at[2], sem.end_a.at[jnp.bitwise_and(k, RING - 1)], me.z_in).start()
 
         @pl.when(me.is_mid)
         def _():
-            wait_for(land.end_b.at[k], sem.end_b.at[k])
+            wait_for(land.end_b.at[k], sem.end_b.at[jnp.bitwise_and(k, RING - 1)])
             packed[k, both] = added(packed[k, both], land.end_b[k])
-            remote(packed.at[k, other], land.mid_b.at[k], send.at[3], sem.mid_b.at[k], me.z_mid).start()
+            remote(packed.at[k, other], land.mid_b.at[k], send.at[3], sem.mid_b.at[jnp.bitwise_and(k, RING - 1)], me.z_mid).start()
 
     def s2(k):
         @pl.when(me.is_mid)
         def _():
-            wait_for(land.end_a.at[k], sem.end_a.at[k])
+            wait_for(land.end_a.at[k], sem.end_a.at[jnp.bitwise_and(k, RING - 1)])
             packed[k, y] = added(packed[k, y], land.end_a[k])
-            remote(packed.at[k, y], land.mid_a.at[k], send.at[4], sem.mid_a.at[k], me.z_mid).start()
-            wait_for(land.mid_b.at[k], sem.mid_b.at[k])
+            remote(packed.at[k, y], land.mid_a.at[k], send.at[4], sem.mid_a.at[jnp.bitwise_and(k, RING - 1)], me.z_mid).start()
+            wait_for(land.mid_b.at[k], sem.mid_b.at[jnp.bitwise_and(k, RING - 1)])
             packed[k, mine] = added(packed[k, mine], land.mid_b[k])
-            remote(packed.at[k, mine], land.rung_b.at[k], send.at[5], sem.rung.at[k], me.y_peer).start()
+            remote(packed.at[k, mine], land.rung_b.at[k], send.at[5], sem.rung.at[jnp.bitwise_and(k, RING - 1)], me.y_peer).start()
 
     def s3(k):
         @pl.when(me.is_mid)
         def _():
-            wait_for(land.mid_a.at[k], sem.mid_a.at[k])
+            wait_for(land.mid_a.at[k], sem.mid_a.at[jnp.bitwise_and(k, RING - 1)])
             total = land.from_y.at[k]
             total[...] = added(packed[k, y], land.mid_a[k])
-            remote(total, out.at[c, k, y], send.at[6], sem.end_final.at[k], me.z_out).start()
-            remote(total, out.at[c, k, y], send.at[7], sem.y_final.at[k], me.y_peer).start()
-            pltpu.make_async_copy(total, out.at[c, k, y], sem.own_a.at[k]).start()
-            wait_for(land.rung_b.at[k], sem.rung.at[k])
+            remote(total, out.at[c, k, y], send.at[6], sem.end_final.at[jnp.bitwise_and(k, RING - 1)], me.z_out).start()
+            remote(total, out.at[c, k, y], send.at[7], sem.y_final.at[jnp.bitwise_and(k, RING - 1)], me.y_peer).start()
+            pltpu.make_async_copy(total, out.at[c, k, y], sem.own_a.at[jnp.bitwise_and(k, RING - 1)]).start()
+            wait_for(land.rung_b.at[k], sem.rung.at[jnp.bitwise_and(k, RING - 1)])
             total = land.end_a.at[k]
             total[...] = added(packed[k, mine], land.rung_b[k])
-            remote(total, out.at[c, k, mine], send.at[8], sem.mid_final.at[k], me.z_mid).start()
-            pltpu.make_async_copy(total, out.at[c, k, mine], sem.own_b.at[k]).start()
+            remote(total, out.at[c, k, mine], send.at[8], sem.mid_final.at[jnp.bitwise_and(k, RING - 1)], me.z_mid).start()
+            pltpu.make_async_copy(total, out.at[c, k, mine], sem.own_b.at[jnp.bitwise_and(k, RING - 1)]).start()
 
     def s4(k):
         @pl.when(me.is_end)
         def _():
-            wait_for(out.at[c, k, y], sem.end_final.at[k])
-            remote(out.at[c, k, y], out.at[c, k, y], send.at[7], sem.y_final.at[k], me.y_peer).start()
+            wait_for(out.at[c, k, y], sem.end_final.at[jnp.bitwise_and(k, RING - 1)])
+            remote(out.at[c, k, y], out.at[c, k, y], send.at[7], sem.y_final.at[jnp.bitwise_and(k, RING - 1)], me.y_peer).start()
 
         @pl.when(me.is_mid)
         def _():
-            wait_for(out.at[c, k, other], sem.mid_final.at[k])
-            wait_for(out.at[c, k, mine], sem.own_b.at[k])
-            remote(out.at[c, k, both], out.at[c, k, both], send.at[9], sem.end_both.at[k], me.z_out).start()
+            wait_for(out.at[c, k, other], sem.mid_final.at[jnp.bitwise_and(k, RING - 1)])
+            wait_for(out.at[c, k, mine], sem.own_b.at[jnp.bitwise_and(k, RING - 1)])
+            remote(out.at[c, k, both], out.at[c, k, both], send.at[9], sem.end_both.at[jnp.bitwise_and(k, RING - 1)], me.z_out).start()
 
     def s5(k):
-        wait_for(out.at[c, k, 1 - y], sem.y_final.at[k])
+        wait_for(out.at[c, k, 1 - y], sem.y_final.at[jnp.bitwise_and(k, RING - 1)])
 
         @pl.when(me.is_end)
         def _():
-            wait_for(out.at[c, k, both], sem.end_both.at[k])
+            wait_for(out.at[c, k, both], sem.end_both.at[jnp.bitwise_and(k, RING - 1)])
 
         @pl.when(me.is_mid)
         def _():
-            wait_for(out.at[c, k, y], sem.own_a.at[k])
-
-        remote(out.at[c, k], out.at[c, k], send.at[10], sem.sibling.at[k], me.sibling).start()
+            wait_for(out.at[c, k, y], sem.own_a.at[jnp.bitwise_and(k, RING - 1)])
+
+        remote(out.at[c, k], out.at[c, k], send.at[10], sem.sibling.at[jnp.bitwise_and(k, RING - 1)], me.sibling).start()
 
     def s6(k):
-        wait_for(out.at[1 - c, k], sem.sibling.at[k])
+        wait_for(out.at[1 - c, k], sem.sibling.at[jnp.bitwise_and(k, RING - 1)])
 
     stages = (s0, s1, s2, s3, s4, s5, s6)
 
@@ -883,7 +885,7 @@
     def _(i):
         slot(start + i)
         for j in range(4):
-            pl.when(i == 4 * (j + 1))(functools.partial(small_step, j))
+            pl.when(i == 3 * (j + 1))(functools.partial(small_step, j))
 
     finish()
     for which in [share_left, share_attention, share_da, share_df] + [share_dz(group) for group in range(groups)]:
@@ -925,7 +927,7 @@
     ]
     scratch += [pltpu.VMEM(shape, dtype) for shape, dtype in others]
     scratch += [section, sections, section, section, section, section]
-    scratch += [dma((steps,))] * 13
+    scratch += [dma((RING,))] * 13
     shares = 4 + n.hidden // width
     scratch += [dma((6,)), dma((2 * n.micro,)), dma((2 * n.micro,)), dma((2 * n.micro,)), dma, dma, dma((shares,)), dma((shares,)), dma((4,)), dma((4,)), dma((11,))]
     return pl.pallas_call(
@@ -938,20 +940,63 @@
     )(content, query, *w, *v)
 
 
+def unpack_kernel(n, packed, smalls, *refs):
+    grads, refs = Weights(*(ref.at[0] for ref in refs[:6])), refs[6:]
+    vectors, table, (block, wide, in_sem, out_sem) = refs[:9], refs[9], refs[10:]
+    width = n.width
+    groups = n.hidden // width
+    places = []
+    for core in range(2):
+        places += [grads.down.at[pl.ds((core * groups // 2 + i) * width, width)] for i in range(groups // 2)]
+        places += [grads.up.at[:, pl.ds((core * groups // 2 + i) * width, width)] for i in range(groups // 2)]
+        places += [grads.value, grads.out] if core else [grads.query, grads.key]
+    count, steps = block.shape[:2]
+    loads = [pltpu.make_async_copy(packed.at[i // (count // 2), pl.ds(i % (count // 2) * steps, steps)], block.at[i], in_sem.at[i]) for i in range(count)]
+    stores = [pltpu.make_async_copy(wide.at[i], place, out_sem.at[i]) for i, place in enumerate(places)]
+    for cp in loads:
+        cp.start()
+    at = 0
+    for vector in vectors:
+        for part in range(vector.shape[1] // width):
+            vector[:, part * width : (part + 1) * width] = smalls[at : at + 1, :]
+            at += 1
+    for h in range(n.heads):
+        table[h] = smalls[12 + h : 13 + h, : n.buckets]
+    rows = block.shape[2] * block.shape[3]
+    for i in range(count):
+        loads[i].wait()
+
+        @pl.loop(0, steps)
+        def _(step):
+            wide[i, pl.ds(pl.multiple_of(step * rows, rows), rows), :] = block[i, step].astype(F32).reshape(rows, width)
+
+        stores[i].start()
+    for cp in stores:
+        cp.wait()
+
+
 def unpack(n, packed, smalls):
-    width, heads = n.width, n.heads
-    groups = n.hidden // width
-    half_down, half_groups = n.hidden // 2, groups // 2
-    halves = [packed[core].reshape(-1, width) for core in range(2)]
-    down = jnp.concatenate([half[:half_down] for half in halves], axis=0).astype(F32)[None]
-    blocks = [[half[half_down + i * width : half_down + (i + 1) * width] for i in range(half_groups + 2)] for half in halves]
-    up = jnp.concatenate(blocks[0][:half_groups] + blocks[1][:half_groups], axis=1).astype(F32)[None]
-    query, key, value, out = (block.astype(F32)[None] for block in blocks[0][half_groups:] + blocks[1][half_groups:])
-    vectors = [smalls[i : i + 1] for i in range(5)]
-    vectors.append(smalls[5 : 5 + groups].reshape(1, n.hidden))
-    vectors += [smalls[i : i + 1] for i in (9, 10, 11)]
-    vectors.append(smalls[12 : 12 + heads, : n.buckets].T[None])
-    return (query, key, value, out, up, down), vectors
+    width, hidden = n.width, n.hidden
+    square, vector = (1, width, width), (1, width)
+    matrices = [square] * 4 + [(1, width, hidden), (1, hidden, width)]
+    vectors = [vector] * 5 + [(1, hidden)] + [vector] * 3
+    vmem, anywhere = pl.BlockSpec(memory_space=pltpu.VMEM), pl.BlockSpec(memory_space=pl.ANY)
+    count = 4 + 2 * hidden // width
+    steps = 2 * packed.shape[1] // count
+    *made, table = pl.pallas_call(
+        functools.partial(unpack_kernel, n),
+        out_shape=[shaped(shape, F32) for shape in matrices + vectors + [(n.heads, 1, n.buckets)]],
+        in_specs=[anywhere, vmem],
+        out_specs=[anywhere] * 6 + [vmem] * 10,
+        scratch_shapes=[
+            pltpu.VMEM((count, steps) + packed.shape[2:], packed.dtype),
+            pltpu.VMEM((count, width, width), F32),
+            pltpu.SemaphoreType.DMA((count,)),
+            pltpu.SemaphoreType.DMA((count,)),
+        ],
+        compiler_params=pltpu.CompilerParams(vmem_limit_bytes=VMEM_LIMIT),
+    )(packed, smalls)
+    return made[:6], made[6:] + [jnp.transpose(table, (1, 2, 0))]
 
 
 def across_blocks(packed, smalls):
@@ -967,7 +1012,7 @@
     micro, seq = position_order.shape
     n = Sizes(micro, seq, query_ends.shape[1] // micro, content_ends.shape[2], rel_table.shape[2], w_up.shape[2], rel_table.shape[1])
     w = Weights(w_query, w_key, w_value, w_out, w_up, w_down)
-    v = Vectors(b_query, b_value, b_out, gain_attn, shift_attn, b_up, b_down, gain_ffn, shift_ffn, rel_table, doc_lengths, position_order)
+    v = Vectors(b_query, b_value, b_out, gain_attn, shift_attn, b_up, b_down, gain_ffn, shift_ffn, jnp.transpose(rel_table, (2, 0, 1)), doc_lengths, position_order)
     content_out, query_out, packed, smalls = run_layers(n, content_ends, query_ends, w, v)
     packed, smalls = across_blocks(packed, smalls)
     g, d = unpack(n, packed, smalls)

time: 260 us -> 242 us (0.931)
  other arithmetic: 14.2 us -> 0 us
  local copies, waits for them, and re-layouts: 13.8 us -> 1.38 us
  Pallas kernels: 231 us -> 240 us
    pallas_call x0 -> x1, Pallas kernels: none -> 15.1 us  [unpack(): pl.pallas_call(functools.partial(unpack_kernel, n), out_shape=[shaped(sha...]
    convert_element_type x4 -> x0, other arithmetic: 14.2 us -> none  [the longest x2 5.39 us: unpack(): block.astype(F32)[None]]
    slice x3 -> x0, local copies, waits for them, and re-layouts: 8.35 us -> none  [the longest x1 4.11 us: unpack(): half[half_down + i * width:half_down + (i + 1) * width]]
    pallas_call x1, Pallas kernels: 231 us -> 225 us  [run_layers(): pl.pallas_call(functools.partial(whole_kernel, n), out_shape=[shaped(cont...]
    unnamed x10 -> x6, local copies, waits for them, and re-layouts: 4.77 us -> 1.38 us
where the time goes in v2:
time: 242 us
  Pallas kernels  240 us (99%)
    pallas_call x1, Pallas kernels, run_layers(): pl.pallas_call(functools.partial(whole_kernel, n), out_shape=[shaped(cont...  225 us
    pallas_call x1, Pallas kernels, unpack(): pl.pallas_call(functools.partial(unpack_kernel, n), out_shape=[shaped(sha...  15.1 us

profile of v2, /device:TPU:0, one launch (start us, length us, event | category | flops | bytes accessed | tf_op | source)
XLA Modules:
  0.0 242.2 jit_solution(18390960547777053727)
XLA Ops:
  0.7 225.0 %shard_map.331 = (bf16[1,256,768]{2,1,0:T(8,128)(2,1)}, bf16[1,32,768]{2,1,0:T(8,128)(2,1)}, bf16[2,72,4,16,768]{4,3,2,1,0:T(8,128)(2,1)}, f32[24,768]{1,0:T(8,128)}) custom-call(bf16[1,256,768]{2,1,0:T(8,128)(2,1)} %refs_0_.1, bf16[1,32,768]{2,1,0:T(8,128)(2,1)} %refs_1_.1, bf16[1,768,768]{2,1,0:T(8,128)(2,1)} %refs_2_.1, bf16[1,768,768]{2,1,0:T(8,128)(2,1)} %refs_3_.1, ...), custom_call_target="tpu_custom_call" | custom-call | tf_op jit(solution)/shard_map/pallas_call | solution.py:933
  225.7 0.0 copy-start
  225.7 0.0 copy-start.1
  225.7 15.1 %shard_map.332 = (f32[1,768,768]{2,1,0:T(8,128)}, f32[1,768,768]{2,1,0:T(8,128)}, f32[1,768,768]{2,1,0:T(8,128)}, f32[1,768,768]{2,1,0:T(8,128)}, f32[1,768,3072...) custom-call(bf16[2,72,4,16,768]{4,3,2,1,0:T(8,128)(2,1)} %get-tuple-, ...), custom_call_target="tpu_custom_call" | custom-call | tf_op jit(solution)/shard_map/pallas_call | solution.py:986
  240.8 0.0 copy-done
  240.8 0.7 copy.40
  241.6 0.0 copy-done.1
  241.6 0.6 copy.41
Async XLA Ops:
  225.7 15.2 %copy-start = (bf16[1,256,768]{2,1,0:T(8,128)(2,1)S(1)}, bf16[1,256,768]{2,1,0:T(8,128)(2,1)}, u32[]{:S(2)}) copy-start(bf16[1,256,768]{2,1,0:T(8,128)(2,1)} %get-tuple-element.76) | copy-start | bytes 1179652
  225.7 15.9 %copy-start.1 = (bf16[1,32,768]{2,1,0:T(8,128)(2,1)S(1)}, bf16[1,32,768]{2,1,0:T(8,128)(2,1)}, u32[]{:S(2)}) copy-start(bf16[1,32,768]{2,1,0:T(8,128)(2,1)} %get-tuple-element.77) | copy-start | bytes 147460

commit v3 on v2

--- a/solution.py
+++ b/solution.py
@@ -21,6 +21,7 @@
 EARLY = 3
 LAG = 2
 RING = 16
+LENT = 8
 CHUNK = 16
 VMEM_LIMIT = 63 * 2**20
 
@@ -133,10 +134,6 @@
 def to_column(row, n):
     shape = (n.seq, n.seq)
     return jnp.sum(jnp.where(iota(shape, 0) == iota(shape, 1), row, 0.0), axis=1, keepdims=True)
-
-
-def picked(order_col, n, place):
-    return order_col[n.seq - n.query :] == place.astype(F32)
 
 
 def bias_and_mask(n, v, bias):
@@ -167,8 +164,8 @@
         doc_col = doc_of(iota((seq, 1), 0).astype(F32))
         unmasked = rank_row < visible_from
         content_sees.append((doc_col == doc_row) & (unmasked | (rank_row <= rank_col)))
-        at_place = picked(order_col, n, iota((query, seq), 1))
         place = order_col[seq - query :]
+        at_place = place == iota((query, seq), 1).astype(F32)
         rank = visible_from + iota((query, 1), 0).astype(F32)
         query_sees.append((doc_of(place) == doc_row) & (unmasked | (rank_row < rank) | at_place))
         chosen.append(jnp.where(at_place, 1.0, 0.0).astype(BF16))
@@ -201,17 +198,19 @@
     return jnp.concatenate([stacked[:half], stacked[half:]], axis=1)
 
 
-def norm_rows(n, summed, spread_ref, gain, shift, write):
+def block_rows(n, b):
+    return pl.ds(pl.multiple_of(b * n.block, 16), n.block)
+
+
+def norm_rows(n, b, summed, normed_ref, spread_ref, gain, shift, write):
     step = n.block // 3
-
-    @pl.loop(0, n.rows // step)
-    def _(i):
-        rows = pl.ds(pl.multiple_of(i * step, step), step)
+    for at in range(0, n.block, step):
+        rows = pl.ds(pl.multiple_of(b * n.block + at, 16), step)
         r = summed[rows, :]
         centered = r - jnp.mean(r, axis=1, keepdims=True)
         spread = lax.rsqrt(jnp.mean(centered * centered, axis=1, keepdims=True) + NORM_EPS)
         normed = centered * spread
-        summed[rows, :] = normed
+        normed_ref[rows, :] = normed
         spread_ref[rows, :] = spread
         write(rows, (normed * gain + shift).astype(BF16))
 
@@ -235,70 +234,70 @@
         )
 
     zero = jnp.zeros((1, n.width), F32)
-    return lax.fori_loop(0, n.rows // step, body, (zero, zero, zero))
-
-
-def project(n, ready, w, v, s):
+    return lax.fori_loop(0, n.rows // step, body, (zero, zero, zero), unroll=3)
+
+
+def project(n, b, ready, w, v, s):
     width, tiles = n.width, n.width // TILE
+    rows = block_rows(n, b)
     for i, matrix in enumerate((w.query, w.key, w.value)):
         ready(i)
-
-        @pl.loop(0, tiles, unroll=True)
-        def _(t):
-            product = dot(s.left[:, :width], matrix[:, cols(t)])
+        for t in range(tiles):
+            at = slice(t * TILE, (t + 1) * TILE)
+            product = dot(s.left[rows, :width], matrix[:, at])
             if i == 0:
-                product = product + v.b_query[:, cols(t)]
+                product = product + v.b_query[:, at]
             if i == 2:
-                product = product + v.b_value[:, cols(t)]
-            s.qkv[:, cols(i * tiles + t)] = product.astype(BF16)
-
-
-def attend(n, s):
+                product = product + v.b_value[:, at]
+            s.qkv[rows, i * width + t * TILE : i * width + (t + 1) * TILE] = product.astype(BF16)
+
+
+def attend(n, b, s):
     factor = (LANES // 2) ** -0.5
-
-    @pl.loop(0, n.micro * n.pairs, unroll=UNROLL)
-    def _(it):
-        b, pair = it // n.pairs, it % n.pairs
-        rows = pl.ds(pl.multiple_of(b * n.block, 16), n.block)
-        keys = pl.ds(pl.multiple_of(b * n.block, 16), n.seq)
-        q = both_heads(s.qkv[rows, cols(pair, LANES)])
-        k = s.qkv[keys, cols(n.pairs + pair, LANES)]
-        val = both_heads(s.qkv[keys, cols(2 * n.pairs + pair, LANES)])
-        scores = dot_nt(q, k) * factor + s.probs[it]
+    rows, keys = block_rows(n, b), pl.ds(pl.multiple_of(b * n.block, 16), n.seq)
+    for pair in range(n.pairs):
+        it = b * n.pairs + pair
+
+        def lanes(part):
+            return slice((part * n.pairs + pair) * LANES, (part * n.pairs + pair + 1) * LANES)
+
+        q = both_heads(s.qkv[rows, lanes(0)])
+        val = both_heads(s.qkv[keys, lanes(2)])
+        scores = dot_nt(q, s.qkv[keys, lanes(1)]) * factor + s.probs[it]
         powers = jnp.exp(scores - jnp.max(scores, axis=1, keepdims=True))
         probs = powers / jnp.sum(powers, axis=1, keepdims=True)
         s.probs[it] = probs
-        mixed = dot(side_by_side(probs.astype(BF16)), val)
-        s.left[rows, cols(n.pairs + pair, LANES)] = mixed.astype(BF16)
-
-
-def attend_out(n, w, v, s):
-    width, tiles = n.width, n.width // TILE
-
-    @pl.loop(0, tiles, unroll=True)
-    def _(t):
-        product = dot(s.left[:, width : 2 * width], w.out[:, cols(t)])
-        s.norm_attn[:, cols(t)] = s.left[:, cols(t)].astype(F32) + product + v.b_out[:, cols(t)]
-
-
-def attend_norm(n, v, s):
+        s.left[rows, lanes(1)] = dot(side_by_side(probs.astype(BF16)), val).astype(BF16)
+
+
+def attend_out(n, b, w, v, s, summed):
+    width = n.width
+    rows = block_rows(n, b)
+    for t in range(width // TILE):
+        at = slice(t * TILE, (t + 1) * TILE)
+        product = dot(s.left[rows, width : 2 * width], w.out[:, at])
+        summed[rows, at] = s.left[rows, at].astype(F32) + product + v.b_out[:, at]
+
+
+def attend_norm(n, b, v, s, summed, copy):
     width = n.width
 
     def keep_h1(rows, value):
         s.left[rows, 2 * width : 3 * width] = value
-
-    norm_rows(n, s.norm_attn, s.spread_attn, v.gain_attn[...], v.shift_attn[...], keep_h1)
-
-
-def go_up(n, w, v, s):
+        copy[rows, :] = value
+
+    norm_rows(n, b, summed, s.norm_attn, s.spread_attn, v.gain_attn[...], v.shift_attn[...], keep_h1)
+
+
+def go_up(n, b, w, v, s, h1):
     width, tiles, left_u = n.width, n.width // TILE, 3 * (n.width // TILE)
     step = n.block // 3
     c = (2 / math.pi) ** 0.5
     staged = s.norm_ffn
 
     def bend(t, i):
-        for at in range(0, n.rows, step):
-            rows = slice(at, at + step)
+        for at in range(0, n.block, step):
+            rows = pl.ds(pl.multiple_of(b * n.block + at, 16), step)
             z = staged[rows, i * TILE : (i + 1) * TILE] + v.b_up[:, cols(t)]
             square = z * z
             half = 0.5 + 0.5 * jnp.tanh(z * (c + 0.044715 * c * square))
@@ -306,46 +305,46 @@
             s.left[rows, cols(left_u + t)] = value.astype(BF16)
             s.slope[rows, cols(t)] = (half + value * (1.0 - half) * (2.0 * c + 0.26829 * c * square)).astype(BF16)
 
-    @pl.loop(0, n.hidden // width)
+    @pl.loop(0, n.hidden // width, unroll=True)
     def _(group):
         for i in range(tiles):
-            staged[:, i * TILE : (i + 1) * TILE] = dot(s.left[:, 2 * width : 3 * width], w.up[:, cols(group * tiles + i)])
+            staged[block_rows(n, b), i * TILE : (i + 1) * TILE] = dot(h1[block_rows(n, b), :], w.up[:, cols(group * tiles + i)])
             if i:
                 bend(group * tiles + i - 1, i - 1)
         bend(group * tiles + tiles - 1, tiles - 1)
 
 
-def go_down(n, w, v, s):
-    width, tiles = n.width, n.width // TILE
-
-    @pl.loop(0, tiles, unroll=True)
-    def _(t):
-        product = dot(s.left[:, 3 * width :], w.down[:, cols(t)])
-        s.norm_ffn[:, cols(t)] = s.left[:, cols(2 * tiles + t)].astype(F32) + product + v.b_down[:, cols(t)]
-
-
-def ffn_norm(n, v, s, y):
+def go_down(n, b, w, v, s, summed):
+    width = n.width
+    rows = block_rows(n, b)
+    for t in range(width // TILE):
+        at = slice(t * TILE, (t + 1) * TILE)
+        h1_at = slice(2 * width + t * TILE, 2 * width + (t + 1) * TILE)
+        product = dot(s.left[rows, 3 * width :], w.down[:, at])
+        summed[rows, at] = s.left[rows, h1_at].astype(F32) + product + v.b_down[:, at]
+
+
+def ffn_norm(n, b, v, s, summed, y):
     def keep_y(rows, value):
         y[rows, :] = value
 
-    norm_rows(n, s.norm_ffn, s.spread_ffn, v.gain_ffn[...], v.shift_ffn[...], keep_y)
-
-
-def ffn_norm_back(n, v, s, dy, right, smalls, resid):
+    norm_rows(n, b, summed, s.norm_ffn, s.spread_ffn, v.gain_ffn[...], v.shift_ffn[...], keep_y)
+
+
+def ffn_norm_back(n, v, s, dy, right, smalls, resid, copy):
     width = n.width
     df_cols = slice(4 * width + n.hidden, 5 * width + n.hidden)
 
     def keep_df(rows, value):
         resid[rows, :] = value
-        right[rows, df_cols] = value.astype(BF16)
+        right[rows, df_cols] = copy[rows, :] = value.astype(BF16)
 
     gain, shift, low = norm_back(n, lambda rows: dy[rows, :].astype(F32), s.norm_ffn, s.spread_ffn, v.gain_ffn[...], keep_df)
     smalls[10:11, :], smalls[11:12, :], smalls[9:10, :] = gain, shift, low
 
 
-def down_back(n, w, s, right, smalls, sent):
+def down_back(n, w, s, right, smalls, df, sent):
     width, tiles = n.width, n.width // TILE
-    df_cols = slice(4 * width + n.hidden, 5 * width + n.hidden)
     step = n.block // 3
     staged = s.norm_ffn
 
@@ -359,10 +358,10 @@
             total = total + jnp.sum(dz.astype(F32).reshape(step // 8, 8, TILE), axis=0)
         smalls[pl.ds(5 + group, 1), cols(i)] = jnp.sum(total, axis=0, keepdims=True)
 
-    @pl.loop(0, n.hidden // width)
+    @pl.loop(0, n.hidden // width, unroll=True)
     def _(group):
         for i in range(tiles):
-            staged[:, i * TILE : (i + 1) * TILE] = dot_nt(right[:, df_cols], w.down[cols(group * tiles + i), :])
+            staged[:, i * TILE : (i + 1) * TILE] = dot_nt(df[...], w.down[cols(group * tiles + i), :])
             if i:
                 bend(group, i - 1)
         bend(group, tiles - 1)
@@ -404,38 +403,35 @@
     square = (n.seq, n.seq)
     same = jnp.where(iota(square, 0) + iota(square, 1) == n.seq - 1, 1.0, 0.0).astype(BF16)
     for b in range(n.micro):
-        order_col = to_column(v.order[b : b + 1, :].astype(F32), n)
-        predicted = picked(order_col, n, n.seq - 1 - iota((n.query, n.seq), 1))
-        chosen[b, : n.seq, :] = same
-        chosen[b, n.seq :, :] = jnp.where(predicted, 1.0, 0.0).astype(BF16)
-
-    @pl.loop(0, n.micro * n.pairs // UNROLL)
-    def _(outside):
-        for inside in range(UNROLL):
-            it = outside * UNROLL + inside
-            b, pair = it // n.pairs, it % n.pairs
-            start = b * n.block
-            rows = pl.ds(pl.multiple_of(start, 16), n.block)
-            keys = pl.ds(pl.multiple_of(start, 16), n.seq)
-            rest = pl.ds(pl.multiple_of(start + n.seq, 16), n.query)
-            grad = both_heads(dy[rows, cols(pair, LANES)])
-            q = both_heads(s.qkv[rows, cols(pair, LANES)])
-            k = both_heads(s.qkv[keys, cols(n.pairs + pair, LANES)])
-            val = s.qkv[keys, cols(2 * n.pairs + pair, LANES)]
-            probs = s.probs[it]
+        place = v.order[b : b + 1, n.seq - n.query :]
+        chosen[b, :, : n.seq] = same
+        chosen[b, :, n.seq :] = jnp.where(place == n.seq - 1 - iota((n.seq, n.query), 0), 1.0, 0.0).astype(BF16)
+
+    @pl.loop(0, n.micro)
+    def _(b):
+        start = b * n.block
+        rows, keys = block_rows(n, b), pl.ds(pl.multiple_of(start, 16), n.seq)
+        rest = pl.ds(pl.multiple_of(start + n.seq, 16), n.query)
+        for pair in range(n.pairs):
+            q_at, k_at, v_at = (slice((part * n.pairs + pair) * LANES, (part * n.pairs + pair + 1) * LANES) for part in range(3))
+            grad = both_heads(dy[rows, q_at])
+            q = both_heads(s.qkv[rows, q_at])
+            k = both_heads(s.qkv[keys, k_at])
+            val = s.qkv[keys, v_at]
+            probs = s.probs[b * n.pairs + pair]
             grad_probs = dot_nt(grad, val)
             inner = jnp.sum(probs * grad_probs, axis=1, keepdims=True)
             grad_scores = (probs * (grad_probs - inner)).astype(BF16)
-            right[rows, cols(pair, LANES)] = (dot(side_by_side(grad_scores), k) * factor).astype(BF16)
-            right[keys, cols(n.pairs + pair, LANES)] = (dot_tn(grad_scores, q) * factor).astype(BF16)
-            right[keys, cols(2 * n.pairs + pair, LANES)] = dot_tn(probs.astype(BF16), grad).astype(BF16)
+            right[rows, q_at] = (dot(side_by_side(grad_scores), k) * factor).astype(BF16)
+            right[keys, k_at] = (dot_tn(grad_scores, q) * factor).astype(BF16)
+            right[keys, v_at] = dot_tn(probs.astype(BF16), grad).astype(BF16)
             none = jnp.zeros((n.query, LANES), BF16)
-            right[rest, cols(n.pairs + pair, LANES)] = none
-            right[rest, cols(2 * n.pairs + pair, LANES)] = none
+            right[rest, k_at] = none
+            right[rest, v_at] = none
             for half in range(2):
                 of_head = grad_scores[half * n.block : (half + 1) * n.block]
-                table_sum[2 * pair + half] += dot_tn(chosen[b], of_head)
-        between(outside)
+                table_sum[2 * pair + half] += dot(chosen[b], of_head)
+        between(b)
 
     smalls[0:1, :] = jnp.sum(right[:, :width].astype(F32), axis=0, keepdims=True)
     smalls[1:2, :] = jnp.sum(right[:, 2 * width : 3 * width].astype(F32), axis=0, keepdims=True)
@@ -490,7 +486,7 @@
             left_tile, group = of(i)
             rhs = right[:, pl.ds(pl.multiple_of(group * n.width, n.width), n.width)]
             product = dot_tn(left[:, cols(left_tile)], rhs).astype(BF16)
-            packed[pl.ds((first + i) * per, per)] = product.reshape((per,) + packed.shape[1:])
+            packed[pl.ds(first + i * per, per)] = product.reshape((per,) + packed.shape[1:])
 
 
 class Landing(NamedTuple):
@@ -516,6 +512,7 @@
     mid_final: Any
     end_both: Any
     sibling: Any
+    back: Any
 
 
 class Place(NamedTuple):
@@ -567,11 +564,12 @@
     @pl.when(me.is_mid)
     def _():
         pl.semaphore_signal(barrier, inc=1, device_id=me.z_mid, device_id_type=MESH)
-        pl.semaphore_wait(barrier, 6)
-
-    @pl.when(me.is_end)
-    def _():
-        pl.semaphore_wait(barrier, 5)
+
+
+def all_here(me):
+    barrier = pltpu.get_barrier_semaphore()
+    pl.when(me.is_mid)(lambda: pl.semaphore_wait(barrier, 6))
+    pl.when(me.is_end)(lambda: pl.semaphore_wait(barrier, 5))
 
 
 def remote(src, dst, send, recv, device):
@@ -586,12 +584,22 @@
     return (a.astype(F32) + b.astype(F32)).astype(BF16)
 
 
-def sums(me, packed, out, land, sem, send):
-    steps = packed.shape[0]
+def sums(me, first, last, borrowed, packed, out, land, sem, send, lent_sem):
+    steps = packed.shape[0] - LENT
+    own = jnp.where(first, steps - LENT, steps + LENT)
+    lent = remote(packed.at[pl.ds(steps - LENT, LENT)], packed.at[pl.ds(borrowed, LENT)], lent_sem.at[0], lent_sem.at[1], me.across)
     c, y, mine, other = me.core, me.y, me.mine, me.other
     both = pl.ds(2, 2)
 
+    def is_lent(k):
+        return last & (k >= borrowed) & (k < borrowed + LENT)
+
+    def row(k):
+        moved = jnp.where(k < borrowed + LENT, steps + k - borrowed, k - LENT)
+        return jnp.where(last & (k >= borrowed), moved, k)
+
     def s0(k):
+        pl.when(last & (k == borrowed))(lent.wait_recv)
         remote(packed.at[k, 1 - y], land.from_y.at[k], send.at[0], sem.y.at[jnp.bitwise_and(k, RING - 1)], me.y_peer).start()
 
         @pl.when(me.is_end)
@@ -623,76 +631,110 @@
             remote(packed.at[k, mine], land.rung_b.at[k], send.at[5], sem.rung.at[jnp.bitwise_and(k, RING - 1)], me.y_peer).start()
 
     def s3(k):
+        o = row(k)
         @pl.when(me.is_mid)
         def _():
             wait_for(land.mid_a.at[k], sem.mid_a.at[jnp.bitwise_and(k, RING - 1)])
             total = land.from_y.at[k]
             total[...] = added(packed[k, y], land.mid_a[k])
-            remote(total, out.at[c, k, y], send.at[6], sem.end_final.at[jnp.bitwise_and(k, RING - 1)], me.z_out).start()
-            remote(total, out.at[c, k, y], send.at[7], sem.y_final.at[jnp.bitwise_and(k, RING - 1)], me.y_peer).start()
-            pltpu.make_async_copy(total, out.at[c, k, y], sem.own_a.at[jnp.bitwise_and(k, RING - 1)]).start()
+            remote(total, out.at[c, o, y], send.at[6], sem.end_final.at[jnp.bitwise_and(k, RING - 1)], me.z_out).start()
+            remote(total, out.at[c, o, y], send.at[7], sem.y_final.at[jnp.bitwise_and(k, RING - 1)], me.y_peer).start()
+            pltpu.make_async_copy(total, out.at[c, o, y], sem.own_a.at[jnp.bitwise_and(k, RING - 1)]).start()
             wait_for(land.rung_b.at[k], sem.rung.at[jnp.bitwise_and(k, RING - 1)])
             total = land.end_a.at[k]
             total[...] = added(packed[k, mine], land.rung_b[k])
-            remote(total, out.at[c, k, mine], send.at[8], sem.mid_final.at[jnp.bitwise_and(k, RING - 1)], me.z_mid).start()
-            pltpu.make_async_copy(total, out.at[c, k, mine], sem.own_b.at[jnp.bitwise_and(k, RING - 1)]).start()
+            remote(total, out.at[c, o, mine], send.at[8], sem.mid_final.at[jnp.bitwise_and(k, RING - 1)], me.z_mid).start()
+            pltpu.make_async_copy(total, out.at[c, o, mine], sem.own_b.at[jnp.bitwise_and(k, RING - 1)]).start()
 
     def s4(k):
+        o = row(k)
         @pl.when(me.is_end)
         def _():
-            wait_for(out.at[c, k, y], sem.end_final.at[jnp.bitwise_and(k, RING - 1)])
-            remote(out.at[c, k, y], out.at[c, k, y], send.at[7], sem.y_final.at[jnp.bitwise_and(k, RING - 1)], me.y_peer).start()
+            wait_for(out.at[c, o, y], sem.end_final.at[jnp.bitwise_and(k, RING - 1)])
+            remote(out.at[c, o, y], out.at[c, o, y], send.at[7], sem.y_final.at[jnp.bitwise_and(k, RING - 1)], me.y_peer).start()
 
         @pl.when(me.is_mid)
         def _():
-            wait_for(out.at[c, k, other], sem.mid_final.at[jnp.bitwise_and(k, RING - 1)])
-            wait_for(out.at[c, k, mine], sem.own_b.at[jnp.bitwise_and(k, RING - 1)])
-            remote(out.at[c, k, both], out.at[c, k, both], send.at[9], sem.end_both.at[jnp.bitwise_and(k, RING - 1)], me.z_out).start()
+            wait_for(out.at[c, o, other], sem.mid_final.at[jnp.bitwise_and(k, RING - 1)])
+            wait_for(out.at[c, o, mine], sem.own_b.at[jnp.bitwise_and(k, RING - 1)])
+            remote(out.at[c, o, both], out.at[c, o, both], send.at[9], sem.end_both.at[jnp.bitwise_and(k, RING - 1)], me.z_out).start()
 
     def s5(k):
-        wait_for(out.at[c, k, 1 - y], sem.y_final.at[jnp.bitwise_and(k, RING - 1)])
-
-        @pl.when(me.is_end)
-        def _():
-            wait_for(out.at[c, k, both], sem.end_both.at[jnp.bitwise_and(k, RING - 1)])
-
-        @pl.when(me.is_mid)
-        def _():
-            wait_for(out.at[c, k, y], sem.own_a.at[jnp.bitwise_and(k, RING - 1)])
-
-        remote(out.at[c, k], out.at[c, k], send.at[10], sem.sibling.at[jnp.bitwise_and(k, RING - 1)], me.sibling).start()
+        o = row(k)
+        @pl.when(k < own)
+        def _():
+            wait_for(out.at[c, o, 1 - y], sem.y_final.at[jnp.bitwise_and(k, RING - 1)])
+
+            @pl.when(me.is_end)
+            def _():
+                wait_for(out.at[c, o, both], sem.end_both.at[jnp.bitwise_and(k, RING - 1)])
+
+            @pl.when(me.is_mid)
+            def _():
+                wait_for(out.at[c, o, y], sem.own_a.at[jnp.bitwise_and(k, RING - 1)])
+
+        @pl.when(k >= own)
+        def _():
+            wait_for(out.at[c, o], sem.back.at[jnp.bitwise_and(k, RING - 1)])
+
+        @pl.when(jnp.logical_not(is_lent(k)))
+        def _():
+            remote(out.at[c, o], out.at[c, o], send.at[10], sem.sibling.at[jnp.bitwise_and(k, RING - 1)], me.sibling).start()
+
+        @pl.when(is_lent(k))
+        def _():
+            home = k - borrowed + steps - LENT
+            remote(out.at[c, o], out.at[c, home], send.at[11], sem.back.at[jnp.bitwise_and(home, RING - 1)], me.across).start()
 
     def s6(k):
-        wait_for(out.at[1 - c, k], sem.sibling.at[jnp.bitwise_and(k, RING - 1)])
+        o = row(k)
+
+        @pl.when(jnp.logical_not(is_lent(k)))
+        def _():
+            wait_for(out.at[1 - c, o], sem.sibling.at[jnp.bitwise_and(k, RING - 1)])
 
     stages = (s0, s1, s2, s3, s4, s5, s6)
+    everything = jnp.where(first, steps, steps + LENT)
+    limits = (own,) * 5 + (everything,) * 2
 
     def slot(t):
         for i, stage in enumerate(stages):
             k = t - i * LAG
 
-            @pl.when((k >= 0) & (k < steps))
+            @pl.when((k >= 0) & (k < limits[i]))
             def _():
-                stage(jnp.clip(k, 0, steps - 1))
-
-    def finish():
-        section = land.from_y
+                stage(jnp.clip(k, 0, steps + LENT - 1))
+
+    def all_sent(count):
+        section, sections = land.from_y.at[pl.ds(0, count)], land.end_b.at[pl.ds(0, count)]
         wait_for(section, send.at[0])
         wait_for(section, send.at[7])
-        wait_for(packed, send.at[10])
 
         @pl.when(me.is_end)
         def _():
-            wait_for(land.end_b, send.at[1])
+            wait_for(sections, send.at[1])
             wait_for(section, send.at[2])
 
         @pl.when(me.is_mid)
         def _():
             for which in (3, 4, 5, 6, 8):
                 wait_for(section, send.at[which])
-            wait_for(land.end_b, send.at[9])
-
-    return slot, steps + (len(stages) - 1) * LAG, finish
+            wait_for(sections, send.at[9])
+
+    def finish():
+        wait_for(packed.at[pl.ds(0, steps)], send.at[10])
+
+        @pl.when(first)
+        def _():
+            all_sent(steps - LENT)
+            lent.wait_send()
+
+        @pl.when(last)
+        def _():
+            all_sent(steps + LENT)
+            wait_for(packed.at[pl.ds(steps, LENT)], send.at[11])
+
+    return slot, steps + LENT + (len(stages) - 1) * LAG, lent.start, finish
 
 
 def small_sums(me, smalls, held, total, recv, send):
@@ -737,8 +779,8 @@
     left, right, y, dx, dy, resid, table_sum, chosen, smalls, held, packed, *refs = refs
     s, refs = State(left.at[pl.ds(0, n.rows)], *refs[:7]), refs[7:]
     land, refs = Landing(*refs[:6]), refs[6:]
-    arrive, refs = Arrival(*refs[:13]), refs[13:]
-    w_sem, in_sem, grad_sem, out_sem, pipe_send, pipe_recv, core_send, core_recv, small_send, small_recv, sum_send = refs
+    arrive, refs = Arrival(*refs[:14]), refs[14:]
+    w_sem, in_sem, grad_sem, out_sem, pipe_send, pipe_recv, core_send, core_recv, small_send, small_recv, sum_send, lent_sem = refs
     width, rows = n.width, n.rows
     inputs = s.left.at[:, pl.ds(0, width)]
     mine_right = right.at[pl.ds(0, rows)]
@@ -760,12 +802,17 @@
         for cp in own_grads:
             cp.start()
 
-    for cp in weights:
+    greet_all(me)
+    for cp in weights[:3]:
         cp.start()
-    greet_all(me)
     bias_and_mask(n, v, s.probs)
-    hand_up = remote(y, inputs, pipe_send, pipe_recv, me.across)
-    hand_down = remote(dx, dy, pipe_send, pipe_recv, me.across)
+    for cp in weights[3:]:
+        cp.start()
+    hand_down = remote(dx, dy, pipe_send.at[n.micro], pipe_recv.at[n.micro], me.across)
+
+    def hand_up(b):
+        return remote(y.at[block_rows(n, b)], inputs.at[block_rows(n, b)], pipe_send.at[b], pipe_recv.at[b], me.across)
+
 
     def to_core(which, src, dst):
         return remote(src, dst, core_send.at[which], core_recv.at[which], me.sibling)
@@ -784,36 +831,36 @@
     def share_dz(group):
         return right_copy(4 + group, pl.multiple_of((4 + group) * width, width), width)
 
-    @pl.when(first)
-    def _():
-        for cp in own_rows:
-            cp.wait()
-
-    @pl.when(last)
-    def _():
-        hand_up.wait_recv()
-
-    done = set()
-
-    def ready(i):
-        if i not in done:
-            done.add(i)
-            weights[i].wait()
-
-    project(n, ready, w, v, s)
-    attend(n, s)
-    ready(3)
-    attend_out(n, w, v, s)
-    attend_norm(n, v, s)
-    ready(4)
-    go_up(n, w, v, s)
-    ready(5)
-    go_down(n, w, v, s)
-    ffn_norm(n, v, s, y)
-
-    @pl.when(first)
-    def _():
-        hand_up.start()
+    @pl.loop(0, n.micro)
+    def _(b):
+        @pl.when(first & (b == 0))
+        def _():
+            for cp in own_rows:
+                cp.wait()
+
+        @pl.when(last)
+        def _():
+            hand_up(b).wait_recv()
+
+        def at_first(i):
+            pl.when(b == 0)(weights[i].wait)
+
+        project(n, b, at_first, w, v, s)
+        attend(n, b, s)
+        at_first(3)
+        attend_out(n, b, w, v, s, resid)
+        attend_norm(n, b, v, s, resid, y)
+        at_first(4)
+        go_up(n, b, w, v, s, y)
+        at_first(5)
+        go_down(n, b, w, v, s, resid)
+        ffn_norm(n, b, v, s, resid, y)
+
+        pl.when(b == 0)(lambda: all_here(me))
+
+        @pl.when(first)
+        def _():
+            hand_up(b).start()
 
     share_left.start()
     results = copies_of([(b, a) for a, b in bucket_rows(n, content_out, query_out, y)], out_sem)
@@ -828,14 +875,16 @@
 
     @pl.when(first)
     def _():
-        hand_up.wait_send()
+        for b in range(n.micro):
+            hand_up(b).wait_send()
         hand_down.wait_recv()
 
-    slot, slots, finish = sums(me, packed, out, land, arrive, sum_send)
+    borrowed = n.hidden // (4 * CHUNK)
+    slot, slots, lend, finish = sums(me, first, last, borrowed, packed, out, land, arrive, sum_send, lent_sem)
     (ffn, ffn_count), (attention, attention_count) = tiles_of(n, me.core)
-    ffn_norm_back(n, v, s, dy, mine_right, smalls, resid)
+    ffn_norm_back(n, v, s, dy, mine_right, smalls, resid, dx)
     share_df.start()
-    down_back(n, w, s, mine_right, smalls, lambda group: share_dz(group).start())
+    down_back(n, w, s, mine_right, smalls, dx, lambda group: share_dz(group).start())
     up_back(n, w, dy, mine_right, resid)
 
     def ffn_grads():
@@ -849,14 +898,14 @@
     attend_norm_back(n, v, s, dy, mine_right, smalls, resid)
     share_da.start()
     out_back(n, w, dy, mine_right)
-    early = n.micro * n.pairs // UNROLL * EARLY
-
-    def between(outside):
+    early = n.micro * EARLY
+
+    def between(b):
         @pl.when(first)
         def _():
             @pl.loop(0, EARLY)
             def _(i):
-                slot(outside * EARLY + i)
+                slot(b * EARLY + i)
 
     attend_back(n, v, s, dy, mine_right, smalls, table_sum, chosen, between)
     share_attention.start()
@@ -878,7 +927,8 @@
     pl.when(last)(ffn_grads)
     share_attention.wait_recv()
     share_da.wait_recv()
-    weight_grads(n, attention, attention_count, ffn_count, left, right, packed)
+    weight_grads(n, attention, attention_count, borrowed + jnp.where(last, LENT, 0), left, right, packed)
+    pl.when(first)(lend)
     start = jnp.where(first, early, 0)
 
     @pl.loop(0, slots - start)
@@ -907,8 +957,9 @@
     vmem, smem, anywhere = (pl.BlockSpec(memory_space=space) for space in (pltpu.VMEM, pltpu.SMEM, pl.ANY))
     dma = pltpu.SemaphoreType.DMA
     steps = (4 * width + 2 * n.hidden) // (2 * 4 * CHUNK)
-    half = (steps, 4, CHUNK, width)
-    section, sections = pltpu.VMEM((steps, CHUNK, width), BF16), pltpu.VMEM((steps, 2, CHUNK, width), BF16)
+    chunks = steps + LENT
+    half = (chunks, 4, CHUNK, width)
+    section, sections = pltpu.VMEM((chunks, CHUNK, width), BF16), pltpu.VMEM((chunks, 2, CHUNK, width), BF16)
     small_shape = (24, width)
     left, *others = state_shapes(n)
     scratch = [pltpu.VMEM(m.shape[1:], BF16) for m in w]
@@ -920,16 +971,16 @@
         pltpu.VMEM((rows, width), BF16),
         pltpu.VMEM((rows, width), F32),
         pltpu.VMEM((n.heads, n.seq, n.seq), F32),
-        pltpu.VMEM((n.micro, n.block, n.seq), BF16),
+        pltpu.VMEM((n.micro, n.seq, n.block), BF16),
         pltpu.VMEM(small_shape, F32),
         pltpu.VMEM((2, 4) + small_shape, F32),
         pltpu.VMEM(half, BF16),
     ]
     scratch += [pltpu.VMEM(shape, dtype) for shape, dtype in others]
     scratch += [section, sections, section, section, section, section]
-    scratch += [dma((RING,))] * 13
+    scratch += [dma((RING,))] * 14
     shares = 4 + n.hidden // width
-    scratch += [dma((6,)), dma((2 * n.micro,)), dma((2 * n.micro,)), dma((2 * n.micro,)), dma, dma, dma((shares,)), dma((shares,)), dma((4,)), dma((4,)), dma((11,))]
+    scratch += [dma((6,)), dma((2 * n.micro,)), dma((2 * n.micro,)), dma((2 * n.micro,)), dma((n.micro + 1,)), dma((n.micro + 1,)), dma((shares,)), dma((shares,)), dma((4,)), dma((4,)), dma((12,)), dma((2,))]
     return pl.pallas_call(
         functools.partial(whole_kernel, n),
         out_shape=[shaped(content.shape), shaped(query.shape), shaped((2,) + half), shaped(small_shape, F32)],
@@ -955,11 +1006,10 @@
     stores = [pltpu.make_async_copy(wide.at[i], place, out_sem.at[i]) for i, place in enumerate(places)]
     for cp in loads:
         cp.start()
-    at = 0
-    for vector in vectors:
+    for i, vector in enumerate(vectors):
         for part in range(vector.shape[1] // width):
+            at = part + (i if i <= 5 else i + 3)
             vector[:, part * width : (part + 1) * width] = smalls[at : at + 1, :]
-            at += 1
     for h in range(n.heads):
         table[h] = smalls[12 + h : 13 + h, : n.buckets]
     rows = block.shape[2] * block.shape[3]
@@ -982,7 +1032,7 @@
     vectors = [vector] * 5 + [(1, hidden)] + [vector] * 3
     vmem, anywhere = pl.BlockSpec(memory_space=pltpu.VMEM), pl.BlockSpec(memory_space=pl.ANY)
     count = 4 + 2 * hidden // width
-    steps = 2 * packed.shape[1] // count
+    steps = 2 * (packed.shape[1] - LENT) // count
     *made, table = pl.pallas_call(
         functools.partial(unpack_kernel, n),
         out_shape=[shaped(shape, F32) for shape in matrices + vectors + [(n.heads, 1, n.buckets)]],

time: 242 us -> 219 us (0.905)
  Pallas kernels: 240 us -> 217 us
    pallas_call x1, Pallas kernels: 225 us -> 202 us  [run_layers(): pl.pallas_call(functools.partial(whole_kernel, n), out_shape=[shaped(cont...]
where the time goes in v3:
time: 219 us
  Pallas kernels  217 us (99%)
    pallas_call x1, Pallas kernels, run_layers(): pl.pallas_call(functools.partial(whole_kernel, n), out_shape=[shaped(cont...  202 us
    pallas_call x1, Pallas kernels, unpack(): pl.pallas_call(functools.partial(unpack_kernel, n), out_shape=[shaped(sha...  15.1 us

profile of v3, /device:TPU:0, one launch (start us, length us, event | category | flops | bytes accessed | tf_op | source)
XLA Modules:
  0.0 219.2 jit_solution(10963951785225666825)
XLA Ops:
  0.7 202.0 %shard_map.331 = (bf16[1,256,768]{2,1,0:T(8,128)(2,1)}, bf16[1,32,768]{2,1,0:T(8,128)(2,1)}, bf16[2,80,4,16,768]{4,3,2,1,0:T(8,128)(2,1)}, f32[24,768]{1,0:T(8,128)}) custom-call(bf16[1,256,768]{2,1,0:T(8,128)(2,1)} %refs_0_.1, bf16[1,32,768]{2,1,0:T(8,128)(2,1)} %refs_1_.1, bf16[1,768,768]{2,1,0:T(8,128)(2,1)} %refs_2_.1, bf16[1,768,768]{2,1,0:T(8,128)(2,1)} %refs_3_.1, ...), custom_call_target="tpu_custom_call" | custom-call | tf_op jit(solution)/shard_map/pallas_call | solution.py:984
  202.7 0.0 copy-start
  202.7 0.0 copy-start.1
  202.7 15.1 %shard_map.332 = (f32[1,768,768]{2,1,0:T(8,128)}, f32[1,768,768]{2,1,0:T(8,128)}, f32[1,768,768]{2,1,0:T(8,128)}, f32[1,768,768]{2,1,0:T(8,128)}, f32[1,768,3072...) custom-call(bf16[2,80,4,16,768]{4,3,2,1,0:T(8,128)(2,1)} %get-tuple-, ...), custom_call_target="tpu_custom_call" | custom-call | tf_op jit(solution)/shard_map/pallas_call | solution.py:1036
  217.8 0.0 copy-done
  217.8 0.7 copy.40
  218.6 0.0 copy-done.1
  218.6 0.6 copy.41
Async XLA Ops:
  202.7 15.2 %copy-start = (bf16[1,256,768]{2,1,0:T(8,128)(2,1)S(1)}, bf16[1,256,768]{2,1,0:T(8,128)(2,1)}, u32[]{:S(2)}) copy-start(bf16[1,256,768]{2,1,0:T(8,128)(2,1)} %get-tuple-element.76) | copy-start | bytes 1179652
  202.7 15.9 %copy-start.1 = (bf16[1,32,768]{2,1,0:T(8,128)(2,1)S(1)}, bf16[1,32,768]{2,1,0:T(8,128)(2,1)}, u32[]{:S(2)}) copy-start(bf16[1,32,768]{2,1,0:T(8,128)(2,1)} %get-tuple-element.77) | copy-start | bytes 147460

commit v4 on v3

--- a/solution.py
+++ b/solution.py
@@ -18,8 +18,10 @@
 TILE = 256
 LANES = 128
 UNROLL = 3
+AHEAD = 4
 EARLY = 3
-LAG = 2
+BESIDE = 1
+OFFSETS = (0, 3, 6, 8, 10, 13, 16)
 RING = 16
 LENT = 8
 CHUNK = 16
@@ -422,15 +424,16 @@
             grad_probs = dot_nt(grad, val)
             inner = jnp.sum(probs * grad_probs, axis=1, keepdims=True)
             grad_scores = (probs * (grad_probs - inner)).astype(BF16)
-            right[rows, q_at] = (dot(side_by_side(grad_scores), k) * factor).astype(BF16)
+            beside = side_by_side(grad_scores)
+            right[rows, q_at] = (dot(beside, k) * factor).astype(BF16)
             right[keys, k_at] = (dot_tn(grad_scores, q) * factor).astype(BF16)
             right[keys, v_at] = dot_tn(probs.astype(BF16), grad).astype(BF16)
             none = jnp.zeros((n.query, LANES), BF16)
             right[rest, k_at] = none
             right[rest, v_at] = none
-            for half in range(2):
-                of_head = grad_scores[half * n.block : (half + 1) * n.block]
-                table_sum[2 * pair + half] += dot(chosen[b], of_head)
+            of_heads = dot(chosen[b], beside)
+            table_sum[2 * pair] += of_heads[:, : n.seq]
+            table_sum[2 * pair + 1] += of_heads[:, n.seq :]
         between(b)
 
     smalls[0:1, :] = jnp.sum(right[:, :width].astype(F32), axis=0, keepdims=True)
@@ -475,7 +478,7 @@
     return (ffn, 2 * down), (attention, 2 * tiles)
 
 
-def weight_grads(n, of, count, first, left, right, packed):
+def weight_grads(n, of, count, first, left, right, packed, between):
     per = TILE // packed.shape[2] // packed.shape[1]
     by = math.gcd(count, UNROLL)
 
@@ -487,6 +490,7 @@
             rhs = right[:, pl.ds(pl.multiple_of(group * n.width, n.width), n.width)]
             product = dot_tn(left[:, cols(left_tile)], rhs).astype(BF16)
             packed[pl.ds(first + i * per, per)] = product.reshape((per,) + packed.shape[1:])
+        between(outside)
 
 
 class Landing(NamedTuple):
@@ -699,7 +703,7 @@
 
     def slot(t):
         for i, stage in enumerate(stages):
-            k = t - i * LAG
+            k = t - OFFSETS[i]
 
             @pl.when((k >= 0) & (k < limits[i]))
             def _():
@@ -734,7 +738,7 @@
             all_sent(steps + LENT)
             wait_for(packed.at[pl.ds(steps, LENT)], send.at[11])
 
-    return slot, steps + LENT + (len(stages) - 1) * LAG, lent.start, finish
+    return slot, steps + LENT + OFFSETS[-1], lent.start, finish
 
 
 def small_sums(me, smalls, held, total, recv, send):
@@ -887,25 +891,37 @@
     down_back(n, w, s, mine_right, smalls, dx, lambda group: share_dz(group).start())
     up_back(n, w, dy, mine_right, resid)
 
+    ffn_steps, attention_steps = (count // math.gcd(count, UNROLL) for count in (ffn_count, attention_count))
+    at_attend = ffn_steps * BESIDE
+    at_attention = at_attend + jnp.where(first, n.micro * EARLY, 0)
+    start = at_attention + attention_steps * BESIDE
+
+    def some_slots(at, count):
+        @pl.loop(0, count)
+        def _(i):
+            slot(at + i)
+
+    def after_ffn(outside):
+        some_slots(outside * BESIDE, BESIDE)
+
+    def after_attention(outside):
+        some_slots(at_attention + outside * BESIDE, BESIDE)
+
     def ffn_grads():
         share_left.wait_recv()
         share_df.wait_recv()
         for group in range(groups):
             share_dz(group).wait_recv()
-        weight_grads(n, ffn, ffn_count, 0, left, right, packed)
+        weight_grads(n, ffn, ffn_count, 0, left, right, packed, after_ffn)
 
     pl.when(first)(ffn_grads)
     attend_norm_back(n, v, s, dy, mine_right, smalls, resid)
     share_da.start()
     out_back(n, w, dy, mine_right)
-    early = n.micro * EARLY
-
     def between(b):
         @pl.when(first)
         def _():
-            @pl.loop(0, EARLY)
-            def _(i):
-                slot(b * EARLY + i)
+            some_slots(at_attend + b * EARLY, EARLY)
 
     attend_back(n, v, s, dy, mine_right, smalls, table_sum, chosen, between)
     share_attention.start()
@@ -915,9 +931,7 @@
     def _():
         hand_down.start()
 
-    table_back(n, smalls, table_sum)
     small_step = small_sums(me, smalls, held, total, small_recv, small_send)
-    small_step(-1)
 
     @pl.when(first)
     def _():
@@ -927,9 +941,10 @@
     pl.when(last)(ffn_grads)
     share_attention.wait_recv()
     share_da.wait_recv()
-    weight_grads(n, attention, attention_count, borrowed + jnp.where(last, LENT, 0), left, right, packed)
+    weight_grads(n, attention, attention_count, borrowed + jnp.where(last, LENT, 0), left, right, packed, after_attention)
     pl.when(first)(lend)
-    start = jnp.where(first, early, 0)
+    table_back(n, smalls, table_sum)
+    small_step(-1)
 
     @pl.loop(0, slots - start)
     def _(i):
@@ -991,9 +1006,10 @@
     )(content, query, *w, *v)
 
 
-def unpack_kernel(n, packed, smalls, *refs):
+def unpack_kernel(n, packed, smalls, content, query, *refs):
+    (content_out, query_out), refs = refs[:2], refs[2:]
     grads, refs = Weights(*(ref.at[0] for ref in refs[:6])), refs[6:]
-    vectors, table, (block, wide, in_sem, out_sem) = refs[:9], refs[9], refs[10:]
+    vectors, table, (block, wide, in_sem, out_sem, row_sem, held_content, held_query) = refs[:9], refs[9], refs[10:]
     width = n.width
     groups = n.hidden // width
     places = []
@@ -1004,7 +1020,11 @@
     count, steps = block.shape[:2]
     loads = [pltpu.make_async_copy(packed.at[i // (count // 2), pl.ds(i % (count // 2) * steps, steps)], block.at[i], in_sem.at[i]) for i in range(count)]
     stores = [pltpu.make_async_copy(wide.at[i], place, out_sem.at[i]) for i, place in enumerate(places)]
-    for cp in loads:
+    rows_in = copies_of([(content, held_content), (query, held_query)], row_sem)
+    rows_back = copies_of([(held_content, content_out), (held_query, query_out)], row_sem)
+    for cp in rows_in:
+        cp.start()
+    for cp in loads[:AHEAD]:
         cp.start()
     for i, vector in enumerate(vectors):
         for part in range(vector.shape[1] // width):
@@ -1015,17 +1035,23 @@
     rows = block.shape[2] * block.shape[3]
     for i in range(count):
         loads[i].wait()
+        if i + AHEAD < count:
+            loads[i + AHEAD].start()
 
         @pl.loop(0, steps)
         def _(step):
             wide[i, pl.ds(pl.multiple_of(step * rows, rows), rows), :] = block[i, step].astype(F32).reshape(rows, width)
 
         stores[i].start()
-    for cp in stores:
+        if i == 0:
+            for back, cp in zip(rows_back, rows_in):
+                cp.wait()
+                back.start()
+    for cp in stores + rows_back:
         cp.wait()
 
 
-def unpack(n, packed, smalls):
+def unpack(n, packed, smalls, content, query):
     width, hidden = n.width, n.hidden
     square, vector = (1, width, width), (1, width)
     matrices = [square] * 4 + [(1, width, hidden), (1, hidden, width)]
@@ -1033,20 +1059,23 @@
     vmem, anywhere = pl.BlockSpec(memory_space=pltpu.VMEM), pl.BlockSpec(memory_space=pl.ANY)
     count = 4 + 2 * hidden // width
     steps = 2 * (packed.shape[1] - LENT) // count
-    *made, table = pl.pallas_call(
+    content, query, *made, table = pl.pallas_call(
         functools.partial(unpack_kernel, n),
-        out_shape=[shaped(shape, F32) for shape in matrices + vectors + [(n.heads, 1, n.buckets)]],
-        in_specs=[anywhere, vmem],
-        out_specs=[anywhere] * 6 + [vmem] * 10,
+        out_shape=[shaped(content.shape), shaped(query.shape)] + [shaped(shape, F32) for shape in matrices + vectors + [(n.heads, 1, n.buckets)]],
+        in_specs=[anywhere, vmem, anywhere, anywhere],
+        out_specs=[anywhere] * 8 + [vmem] * 10,
         scratch_shapes=[
             pltpu.VMEM((count, steps) + packed.shape[2:], packed.dtype),
             pltpu.VMEM((count, width, width), F32),
             pltpu.SemaphoreType.DMA((count,)),
             pltpu.SemaphoreType.DMA((count,)),
+            pltpu.SemaphoreType.DMA((2,)),
+            pltpu.VMEM(content.shape, BF16),
+            pltpu.VMEM(query.shape, BF16),
         ],
         compiler_params=pltpu.CompilerParams(vmem_limit_bytes=VMEM_LIMIT),
-    )(packed, smalls)
-    return made[:6], made[6:] + [jnp.transpose(table, (1, 2, 0))]
+    )(packed, smalls, content, query)
+    return content, query, made[:6], made[6:] + [jnp.transpose(table, (1, 2, 0))]
 
 
 def across_blocks(packed, smalls):
@@ -1065,7 +1094,7 @@
     v = Vectors(b_query, b_value, b_out, gain_attn, shift_attn, b_up, b_down, gain_ffn, shift_ffn, jnp.transpose(rel_table, (2, 0, 1)), doc_lengths, position_order)
     content_out, query_out, packed, smalls = run_layers(n, content_ends, query_ends, w, v)
     packed, smalls = across_blocks(packed, smalls)
-    g, d = unpack(n, packed, smalls)
+    content_out, query_out, g, d = unpack(n, packed, smalls, content_out, query_out)
     return content_out, query_out, g[0], d[0], g[1], g[2], d[1], g[3], d[2], d[3], d[4], g[4], d[5], g[5], d[6], d[7], d[8], d[9]
 
 

time: 219 us -> 210 us (0.959)
  Pallas kernels: 217 us -> 208 us
    pallas_call x1, Pallas kernels: 202 us -> 192 us  [run_layers(): pl.pallas_call(functools.partial(whole_kernel, n), out_shape=[shaped(cont...]
where the time goes in v4:
time: 210 us; the launch traced here: 209 us
  Pallas kernels  208 us (99%)
    pallas_call x1, Pallas kernels, run_layers(): pl.pallas_call(functools.partial(whole_kernel, n), out_shape=[shaped(cont...  192 us
    pallas_call x1, Pallas kernels, unpack(): pl.pallas_call(functools.partial(unpack_kernel, n), out_shape=[shaped(con...  15.6 us

profile of v4, /device:TPU:0, one launch (start us, length us, event | category | flops | bytes accessed | tf_op | source)
XLA Modules:
  0.0 208.9 jit_solution(1559981927770747757)
XLA Ops:
  0.7 192.5 %shard_map.331 = (bf16[1,256,768]{2,1,0:T(8,128)(2,1)}, bf16[1,32,768]{2,1,0:T(8,128)(2,1)}, bf16[2,80,4,16,768]{4,3,2,1,0:T(8,128)(2,1)}, f32[24,768]{1,0:T(8,128)}) custom-call(bf16[1,256,768]{2,1,0:T(8,128)(2,1)} %refs_0_.1, bf16[1,32,768]{2,1,0:T(8,128)(2,1)} %refs_1_.1, bf16[1,768,768]{2,1,0:T(8,128)(2,1)} %refs_2_.1, bf16[1,768,768]{2,1,0:T(8,128)(2,1)} %refs_3_.1, ...), custom_call_target="tpu_custom_call" | custom-call | tf_op jit(solution)/shard_map/pallas_call | solution.py:999
  193.2 15.6 %shard_map.332 = (bf16[1,256,768]{2,1,0:T(8,128)(2,1)}, bf16[1,32,768]{2,1,0:T(8,128)(2,1)}, f32[1,768,768]{2,1,0:T(8,128)}, f32[1,768,768]{2,1,0:T(8,128)}, f32...) custom-call(bf16[2,80,4,16,768]{4,3,2,1,0:T(8,128)(2,1)} %get-tuple-, ...), custom_call_target="tpu_custom_call" | custom-call | tf_op jit(solution)/shard_map/pallas_call | solution.py:1062

commit v5 on v4

--- a/solution.py
+++ b/solution.py
@@ -17,7 +17,7 @@
 THRESHOLDS = (12, 16, 23, 32, 46, 64, 91)
 TILE = 256
 LANES = 128
-UNROLL = 3
+UNROLL = 1
 AHEAD = 4
 EARLY = 3
 BESIDE = 1
@@ -889,9 +889,8 @@
     ffn_norm_back(n, v, s, dy, mine_right, smalls, resid, dx)
     share_df.start()
     down_back(n, w, s, mine_right, smalls, dx, lambda group: share_dz(group).start())
-    up_back(n, w, dy, mine_right, resid)
-
-    ffn_steps, attention_steps = (count // math.gcd(count, UNROLL) for count in (ffn_count, attention_count))
+
+    ffn_steps, attention_steps = (count // math.gcd(ffn_count // 2, UNROLL) for count in (ffn_count, attention_count))
     at_attend = ffn_steps * BESIDE
     at_attention = at_attend + jnp.where(first, n.micro * EARLY, 0)
     start = at_attention + attention_steps * BESIDE
@@ -910,11 +909,15 @@
     def ffn_grads():
         share_left.wait_recv()
         share_df.wait_recv()
+        half = ffn_count // 2
+        weight_grads(n, ffn, half, 0, left, right, packed, after_ffn)
         for group in range(groups):
             share_dz(group).wait_recv()
-        weight_grads(n, ffn, ffn_count, 0, left, right, packed, after_ffn)
+        per = TILE // (4 * CHUNK)
+        weight_grads(n, lambda i: ffn(half + i), half, half * per, left, right, packed, lambda i: after_ffn(ffn_steps // 2 + i))
 
     pl.when(first)(ffn_grads)
+    up_back(n, w, dy, mine_right, resid)
     attend_norm_back(n, v, s, dy, mine_right, smalls, resid)
     share_da.start()
     out_back(n, w, dy, mine_right)

time: 210 us -> 209 us (level)
  no operation moved by 1% of the time
where the time goes in v5:
time: 209 us; the launch traced here: 208 us
  Pallas kernels  207 us (99%)
    pallas_call x1, Pallas kernels, run_layers(): pl.pallas_call(functools.partial(whole_kernel, n), out_shape=[shaped(cont...  192 us
    pallas_call x1, Pallas kernels, unpack(): pl.pallas_call(functools.partial(unpack_kernel, n), out_shape=[shaped(con...  15.6 us

profile of v5, /device:TPU:0, one launch (start us, length us, event | category | flops | bytes accessed | tf_op | source)
XLA Modules:
  0.0 208.3 jit_solution(8569776834816715793)
XLA Ops:
  0.7 191.8 %shard_map.331 = (bf16[1,256,768]{2,1,0:T(8,128)(2,1)}, bf16[1,32,768]{2,1,0:T(8,128)(2,1)}, bf16[2,80,4,16,768]{4,3,2,1,0:T(8,128)(2,1)}, f32[24,768]{1,0:T(8,128)}) custom-call(bf16[1,256,768]{2,1,0:T(8,128)(2,1)} %refs_0_.1, bf16[1,32,768]{2,1,0:T(8,128)(2,1)} %refs_1_.1, bf16[1,768,768]{2,1,0:T(8,128)(2,1)} %refs_2_.1, bf16[1,768,768]{2,1,0:T(8,128)(2,1)} %refs_3_.1, ...), custom_call_target="tpu_custom_call" | custom-call | tf_op jit(solution)/shard_map/pallas_call | solution.py:1002
  192.5 15.6 %shard_map.332 = (bf16[1,256,768]{2,1,0:T(8,128)(2,1)}, bf16[1,32,768]{2,1,0:T(8,128)(2,1)}, f32[1,768,768]{2,1,0:T(8,128)}, f32[1,768,768]{2,1,0:T(8,128)}, f32...) custom-call(bf16[2,80,4,16,768]{4,3,2,1,0:T(8,128)(2,1)} %get-tuple-, ...), custom_call_target="tpu_custom_call" | custom-call | tf_op jit(solution)/shard_map/pallas_call | solution.py:1065

commit v6 on v5

--- a/solution.py
+++ b/solution.py
@@ -604,14 +604,14 @@
 
     def s0(k):
         pl.when(last & (k == borrowed))(lent.wait_recv)
-        remote(packed.at[k, 1 - y], land.from_y.at[k], send.at[0], sem.y.at[jnp.bitwise_and(k, RING - 1)], me.y_peer).start()
+        remote(packed.at[k, 1 - y], land.from_y.at[k], send.at[0], sem.y.at[jnp.bitwise_and(k, RING // 2 - 1)], me.y_peer).start()
 
         @pl.when(me.is_end)
         def _():
             remote(packed.at[k, both], land.end_b.at[k], send.at[1], sem.end_b.at[jnp.bitwise_and(k, RING - 1)], me.z_in).start()
 
     def s1(k):
-        wait_for(land.from_y.at[k], sem.y.at[jnp.bitwise_and(k, RING - 1)])
+        wait_for(land.from_y.at[k], sem.y.at[jnp.bitwise_and(k, RING // 2 - 1)])
         packed[k, y] = added(packed[k, y], land.from_y[k])
 
         @pl.when(me.is_end)
@@ -622,33 +622,33 @@
         def _():
             wait_for(land.end_b.at[k], sem.end_b.at[jnp.bitwise_and(k, RING - 1)])
             packed[k, both] = added(packed[k, both], land.end_b[k])
-            remote(packed.at[k, other], land.mid_b.at[k], send.at[3], sem.mid_b.at[jnp.bitwise_and(k, RING - 1)], me.z_mid).start()
+            remote(packed.at[k, other], land.mid_b.at[k], send.at[3], sem.mid_b.at[jnp.bitwise_and(k, RING // 2 - 1)], me.z_mid).start()
 
     def s2(k):
         @pl.when(me.is_mid)
         def _():
             wait_for(land.end_a.at[k], sem.end_a.at[jnp.bitwise_and(k, RING - 1)])
             packed[k, y] = added(packed[k, y], land.end_a[k])
-            remote(packed.at[k, y], land.mid_a.at[k], send.at[4], sem.mid_a.at[jnp.bitwise_and(k, RING - 1)], me.z_mid).start()
-            wait_for(land.mid_b.at[k], sem.mid_b.at[jnp.bitwise_and(k, RING - 1)])
+            remote(packed.at[k, y], land.mid_a.at[k], send.at[4], sem.mid_a.at[jnp.bitwise_and(k, RING // 2 - 1)], me.z_mid).start()
+            wait_for(land.mid_b.at[k], sem.mid_b.at[jnp.bitwise_and(k, RING // 2 - 1)])
             packed[k, mine] = added(packed[k, mine], land.mid_b[k])
-            remote(packed.at[k, mine], land.rung_b.at[k], send.at[5], sem.rung.at[jnp.bitwise_and(k, RING - 1)], me.y_peer).start()
+            remote(packed.at[k, mine], land.rung_b.at[k], send.at[5], sem.rung.at[jnp.bitwise_and(k, RING // 2 - 1)], me.y_peer).start()
 
     def s3(k):
         o = row(k)
         @pl.when(me.is_mid)
         def _():
-            wait_for(land.mid_a.at[k], sem.mid_a.at[jnp.bitwise_and(k, RING - 1)])
+            wait_for(land.mid_a.at[k], sem.mid_a.at[jnp.bitwise_and(k, RING // 2 - 1)])
             total = land.from_y.at[k]
             total[...] = added(packed[k, y], land.mid_a[k])
             remote(total, out.at[c, o, y], send.at[6], sem.end_final.at[jnp.bitwise_and(k, RING - 1)], me.z_out).start()
             remote(total, out.at[c, o, y], send.at[7], sem.y_final.at[jnp.bitwise_and(k, RING - 1)], me.y_peer).start()
-            pltpu.make_async_copy(total, out.at[c, o, y], sem.own_a.at[jnp.bitwise_and(k, RING - 1)]).start()
-            wait_for(land.rung_b.at[k], sem.rung.at[jnp.bitwise_and(k, RING - 1)])
+            pltpu.make_async_copy(total, out.at[c, o, y], sem.own_a.at[jnp.bitwise_and(k, RING // 2 - 1)]).start()
+            wait_for(land.rung_b.at[k], sem.rung.at[jnp.bitwise_and(k, RING // 2 - 1)])
             total = land.end_a.at[k]
             total[...] = added(packed[k, mine], land.rung_b[k])
-            remote(total, out.at[c, o, mine], send.at[8], sem.mid_final.at[jnp.bitwise_and(k, RING - 1)], me.z_mid).start()
-            pltpu.make_async_copy(total, out.at[c, o, mine], sem.own_b.at[jnp.bitwise_and(k, RING - 1)]).start()
+            remote(total, out.at[c, o, mine], send.at[8], sem.mid_final.at[jnp.bitwise_and(k, RING // 2 - 1)], me.z_mid).start()
+            pltpu.make_async_copy(total, out.at[c, o, mine], sem.own_b.at[jnp.bitwise_and(k, RING // 2 - 1)]).start()
 
     def s4(k):
         o = row(k)
@@ -659,8 +659,8 @@
 
         @pl.when(me.is_mid)
         def _():
-            wait_for(out.at[c, o, other], sem.mid_final.at[jnp.bitwise_and(k, RING - 1)])
-            wait_for(out.at[c, o, mine], sem.own_b.at[jnp.bitwise_and(k, RING - 1)])
+            wait_for(out.at[c, o, other], sem.mid_final.at[jnp.bitwise_and(k, RING // 2 - 1)])
+            wait_for(out.at[c, o, mine], sem.own_b.at[jnp.bitwise_and(k, RING // 2 - 1)])
             remote(out.at[c, o, both], out.at[c, o, both], send.at[9], sem.end_both.at[jnp.bitwise_and(k, RING - 1)], me.z_out).start()
 
     def s5(k):
@@ -675,11 +675,11 @@
 
             @pl.when(me.is_mid)
             def _():
-                wait_for(out.at[c, o, y], sem.own_a.at[jnp.bitwise_and(k, RING - 1)])
+                wait_for(out.at[c, o, y], sem.own_a.at[jnp.bitwise_and(k, RING // 2 - 1)])
 
         @pl.when(k >= own)
         def _():
-            wait_for(out.at[c, o], sem.back.at[jnp.bitwise_and(k, RING - 1)])
+            wait_for(out.at[c, o], sem.back.at[jnp.bitwise_and(k, RING // 2 - 1)])
 
         @pl.when(jnp.logical_not(is_lent(k)))
         def _():
@@ -688,7 +688,7 @@
         @pl.when(is_lent(k))
         def _():
             home = k - borrowed + steps - LENT
-            remote(out.at[c, o], out.at[c, home], send.at[11], sem.back.at[jnp.bitwise_and(home, RING - 1)], me.across).start()
+            remote(out.at[c, o], out.at[c, home], send.at[11], sem.back.at[jnp.bitwise_and(home, RING // 2 - 1)], me.across).start()
 
     def s6(k):
         o = row(k)
@@ -996,7 +996,8 @@
     ]
     scratch += [pltpu.VMEM(shape, dtype) for shape, dtype in others]
     scratch += [section, sections, section, section, section, section]
-    scratch += [dma((RING,))] * 14
+    halved = (0, 3, 4, 5, 6, 7, 10, 13)
+    scratch += [dma((RING // 2 if i in halved else RING,)) for i in range(14)]
     shares = 4 + n.hidden // width
     scratch += [dma((6,)), dma((2 * n.micro,)), dma((2 * n.micro,)), dma((2 * n.micro,)), dma((n.micro + 1,)), dma((n.micro + 1,)), dma((shares,)), dma((shares,)), dma((4,)), dma((4,)), dma((12,)), dma((2,))]
     return pl.pallas_call(

time: 209 us -> 208 us (level)
  no operation moved by 1% of the time
where the time goes in v6:
time: 208 us
  Pallas kernels  207 us (100%)
    pallas_call x1, Pallas kernels, run_layers(): pl.pallas_call(functools.partial(whole_kernel, n), out_shape=[shaped(cont...  191 us
    pallas_call x1, Pallas kernels, unpack(): pl.pallas_call(functools.partial(unpack_kernel, n), out_shape=[shaped(con...  15.6 us

profile of v6, /device:TPU:0, one launch (start us, length us, event | category | flops | bytes accessed | tf_op | source)
XLA Modules:
  0.0 207.7 jit_solution(16072892814586487989)
XLA Ops:
  0.7 191.3 %shard_map.331 = (bf16[1,256,768]{2,1,0:T(8,128)(2,1)}, bf16[1,32,768]{2,1,0:T(8,128)(2,1)}, bf16[2,80,4,16,768]{4,3,2,1,0:T(8,128)(2,1)}, f32[24,768]{1,0:T(8,128)}) custom-call(bf16[1,256,768]{2,1,0:T(8,128)(2,1)} %refs_0_.1, bf16[1,32,768]{2,1,0:T(8,128)(2,1)} %refs_1_.1, bf16[1,768,768]{2,1,0:T(8,128)(2,1)} %refs_2_.1, bf16[1,768,768]{2,1,0:T(8,128)(2,1)} %refs_3_.1, ...), custom_call_target="tpu_custom_call" | custom-call | tf_op jit(solution)/shard_map/pallas_call | solution.py:1003
  192.0 15.6 %shard_map.332 = (bf16[1,256,768]{2,1,0:T(8,128)(2,1)}, bf16[1,32,768]{2,1,0:T(8,128)(2,1)}, f32[1,768,768]{2,1,0:T(8,128)}, f32[1,768,768]{2,1,0:T(8,128)}, f32...) custom-call(bf16[2,80,4,16,768]{4,3,2,1,0:T(8,128)(2,1)} %get-tuple-, ...), custom_call_target="tpu_custom_call" | custom-call | tf_op jit(solution)/shard_map/pallas_call | solution.py:1066
